TPU v7x, 32 devices: a whole 2x2x4 slice. The times are simulated.
32 devices in a mesh: seq: 16 (over z, y, x), head: 2 (over core).
Axes of the slice: x: 2, y: 2, z: 4, core: 2. Of those that a mesh axis runs over, the one named last changes fastest.
Arguments:
- stream_x: bfloat16 [4096, 3072], P('seq', 'head')
- qkv_weight: bfloat16 [3072, 4608], P(None, 'head')
- short_lengths: int32 [8], replicated, may hold values from 1 to 256, 1024 in all
- cache_owner: int32 [4096, 1], P('seq'), may hold values from 0 to 15, as said below
Outputs:
- attended: bfloat16 [4096, 1536], P('seq', 'head')
- row_lse: float32 [16, 4096], P('head', 'seq')
- kv_cache: bfloat16 [8192, 3072], P('seq', 'head')
Inputs may be any that keep to these rules, and one draw needn't show every extreme that they name: `short_lengths`: the lengths sum to 1024 and the longest is exactly 256. `cache_owner`: the rows of one device form 256 / 32 aligned pages of 32 rows; all rows of a page name the same owner, and the pages of one device name different owners, so an owner takes either none or exactly 32 rows of one device.
All inputs are finite; a program needn't handle non-finite values.
Results may differ from a plain program's by a relative error of at most 0.0083.
Values may be sent and summed in bfloat16 or wider, within the bound.
A program may use at most 128 MiB of HBM per device.

v0:
```python
import math

import jax
import jax.numpy as jnp
from jax import lax
from jax.sharding import PartitionSpec as P

HD = 96


neg_large = -1e30
rope_base = 10000.0


def boundaries(short_lengths, long_length):
    running = jnp.cumsum(short_lengths)
    return jnp.concatenate([jnp.zeros((1,), jnp.int32), running]) + long_length


def locate(row_ids, bounds):
    passed = row_ids[:, None] >= bounds[None, :]
    segment = jnp.sum(passed.astype(jnp.int32), axis=1)
    seg_begin = jnp.max(jnp.where(passed, bounds[None, :], 0), axis=1)
    return (segment, seg_begin)


def rotate(parts, position, head_dim):
    half_dim = head_dim // 2
    inverse_freq = rope_base ** (-jnp.arange(half_dim, dtype=jnp.float32) / half_dim)
    angle = position[:, None, None] * inverse_freq[None, None, :]
    cosine = jnp.cos(angle)
    sine_part = jnp.sin(angle)
    first_half = parts[..., :half_dim]
    second_half = parts[..., half_dim:]
    return jnp.concatenate(
        [
            first_half * cosine - second_half * sine_part,
            second_half * cosine + first_half * sine_part,
        ],
        axis=-1,
    )


def body(stream_x, qkv_weight, short_lengths, cache_owner):
    seq_count = lax.axis_size("seq")
    tok_count = stream_x.shape[0]
    heads_here = qkv_weight.shape[1] // (3 * HD)
    long_length = tok_count * (seq_count * 11 // 16)
    bounds = boundaries(short_lengths, long_length)
    pad_segment = short_lengths.shape[0] + 1
    first_row = lax.axis_index("seq") * tok_count
    row_ids = first_row + jnp.arange(tok_count, dtype=jnp.int32)
    segment, seg_begin = locate(row_ids, bounds)
    position = (row_ids - seg_begin).astype(jnp.float32)
    is_padding = segment == pad_segment
    projected = jnp.dot(
        lax.all_gather(stream_x, "head", axis=1, tiled=True),
        qkv_weight,
        preferred_element_type=jnp.float32,
    )
    projected = projected.reshape(tok_count, heads_here, 3, HD)
    queries = rotate(projected[:, :, 0], position, HD).astype(jnp.bfloat16)
    rotated_keys = rotate(projected[:, :, 1], position, HD).astype(jnp.bfloat16)
    values = projected[:, :, 2].astype(jnp.bfloat16)
    packed = jnp.stack([rotated_keys, values], axis=2).reshape(tok_count, heads_here * 2 * HD)
    score_scale = 1.0 / math.sqrt(HD)
    shard_piece = lax.all_gather(packed, "seq", axis=0, tiled=True)
    key_count = shard_piece.shape[0]
    key_ids = jnp.arange(key_count, dtype=jnp.int32)
    row_max = jnp.full((heads_here, tok_count), neg_large, jnp.float32)
    key_segment, unused = locate(key_ids, bounds)
    key_value = shard_piece.reshape(key_count, heads_here, 2, HD)
    scores = (
        jnp.einsum("qhe,khe->hqk", queries, key_value[:, :, 0], preferred_element_type=jnp.float32)
        * score_scale
    )
    allowed = (
        (key_segment[None, :] == segment[:, None])
        & (key_ids[None, :] <= row_ids[:, None])
        & (key_ids[None, :] >= 0)
    )
    new_max = jnp.maximum(row_max, jnp.max(jnp.where(allowed[None], scores, neg_large), axis=2))
    weights = jnp.where(allowed[None], jnp.exp(scores - new_max[:, :, None]), 0.0)
    denominator = jnp.sum(weights, axis=2)
    context = jnp.einsum(
        "hqk,khe->hqe",
        weights.astype(jnp.bfloat16),
        key_value[:, :, 1],
        preferred_element_type=jnp.float32,
    )
    running = (new_max, denominator, context)
    row_max, denominator, context = running
    context = context / denominator[:, :, None]
    row_lse = jnp.where(is_padding[None, :], 0.0, row_max + jnp.log(denominator))
    context = jnp.where(is_padding[None, :, None], 0.0, context)
    attended = (
        jnp.transpose(context, (1, 0, 2)).reshape(tok_count, heads_here * HD).astype(jnp.bfloat16)
    )
    capacity = 2 * tok_count // seq_count
    owner_ids = cache_owner[:, 0]
    one_hot = (owner_ids[:, None] == jnp.arange(seq_count, dtype=jnp.int32)[None, :]).astype(
        jnp.int32
    )
    owner_rank = jnp.sum(jnp.cumsum(one_hot, axis=0) * one_hot, axis=1) - 1
    slot_index = owner_ids * capacity + owner_rank
    cached = jnp.where(is_padding[:, None], jnp.zeros_like(packed), packed)
    outbox = (
        jnp.zeros((seq_count * capacity, packed.shape[1]), jnp.bfloat16).at[slot_index].set(cached)
    )
    received = lax.all_to_all(
        outbox.reshape(seq_count, capacity, packed.shape[1]),
        "seq",
        split_axis=0,
        concat_axis=0,
        tiled=True,
    )
    kv_cache = received.reshape(seq_count * capacity, packed.shape[1])
    return (attended, row_lse, kv_cache)


def solution(mesh):
    return jax.shard_map(
        body,
        mesh=mesh,
        in_specs=(P("seq", "head"), P(None, "head"), P(), P("seq", None)),
        out_specs=(P("seq", "head"), P("head", "seq"), P("seq", "head")),
        check_vma=False,
    )
```

profile of v0, /device:TPU:20, one launch (start us, length us, event | category | flops | bytes accessed | tf_op | source)
XLA Modules:
  0.0 294.1 jit_solution(992214842635756070)
XLA Ops:
  7.2 0.7 all-gather.3.cloned.1.call-update
  7.9 0.8 reduce-window.18
  9.0 0.3 multiply_cosine_fusion
  9.2 11.4 %all-gather.3.cloned.1.call-done = bf16[256,3072]{1,0:T(8,128)(2,1)} async-done(((bf16[256,1536]{1,0:T(8,128)(2,1)}), bf16[256,3072]{1,0:T(8,128)(2,1)}) %all-gather.3.cloned.1.call-update) | async-done | bytes 1572880 | tf_op jit(solution)/shard_map/all_gather | solution.py:57
  20.7 9.2 %fusion.35 = f32[256,2304]{0,1:T(8,128)S(1)} fusion(bf16[256,3072]{1,0:T(8,128)(2,1)} %all-gather.3.cloned.1.call-done, bf16[3072,2304]{1,0:T(8,128)(2,1)} %param.5), kind=kOutput, calls=%fused_computation.61 | convolution fusion | flops 3623878656 | bytes 18087936 | tf_op jit(solution)/shard_map/dot_general | solution.py:56
  29.9 0.1 fusion.34
  30.1 0.1 copy_bitcast_fusion
  30.2 0.3 subtract_convert_fusion.1
  30.6 0.9 copy.34
  31.6 0.6 reduce-window.19
  32.1 0.2 slice_reduce_fusion
  32.5 1.2 broadcast_select_fusion
  33.7 0.3 copy.38
  34.0 3.1 %scatter_custom_fusion = bf16[512,1536]{1,0:T(8,128)(2,1)} fusion(s32[256]{0:T(256)S(1)} %bitcast.78, bf16[256,1536]{1,0:T(8,128)(2,1)S(1)} %copy.38, bf16[]{:T(256)} %constant.50.clone.1), kind=kCustom, calls=%fused_computation.20 | custom fusion | bytes 1572866 | tf_op jit(solution)/shard_map/scatter | solution.py:108
  37.1 6.9 %all-to-all-start = ((bf16[16,32,1536]{2,1,0:T(8,128)(2,1)}), bf16[16,32,1536]{2,1,0:T(8,128)(2,1)S(1)}, u32[]{:S(2)}, u32[]{:S(2)}) async-start(bf16[16,32,1536]{2,1,0:T(8,128)(2,1)} %bitcast.19), calls=%async_computation | async-start | bytes 3145728 | tf_op jit(solution)/shard_map/all_to_all | solution.py:110
  44.2 1.3 fusion.6
  45.5 44.3 %all-to-all-done = bf16[16,32,1536]{2,1,0:T(8,128)(2,1)S(1)} async-done(((bf16[16,32,1536]{2,1,0:T(8,128)(2,1)}), bf16[16,32,1536]{2,1,0:T(8,128)(2,1)S(1)}, u32[]{:S(2)}, u32[]{:S(2)}) %all-to-all-start) | async-done | bytes 1572896 | tf_op jit(solution)/shard_map/all_to_all | solution.py:110
  89.8 147.1 %all-gather.5.cloned.1.call-done = bf16[4096,1536]{0,1:T(8,128)(2,1)} async-done(((bf16[256,1536]{0,1:T(8,128)(2,1)}), bf16[4096,1536]{0,1:T(8,128)(2,1)}) %all-gather.5.cloned.1.call-update) | async-done | bytes 12582928 | tf_op jit(solution)/shard_map/all_gather | solution.py:67
  236.8 17.1 %select_reduce_fusion = (f32[8,256]{1,0:T(8,128)S(1)}, f32[8,256,4096]{2,1,0:T(8,128)}) fusion(pred[256,4096]{1,0:T(8,128)(4,1)S(1)} %fusion.6, bf16[4096,8,2,96]{0,3,2,1:T(8,128)(2,1)} %bitcast.69, bf16[256,8,48]{0,2,1:T(8,128)(2,1)S(1)} %get-tuple-element.20, bf16[256,8,48]{0,2,1:T(8,128)(2,1)S(1)} %get-tuple-element.19), kind=kOutput, calls=%fused_computation.2 | convolution fusion | flops 1636562944 | bytes 41295872 | tf_op jit(solution)/shard_map/qhe,khe->hqk/dot_general | solution.py:74
  253.9 15.5 %fusion = f32[8,256]{1,0:T(8,128)S(1)} fusion(f32[8,256,4096]{2,1,0:T(8,128)} %get-tuple-element.28, f32[8,256]{1,0:T(8,128)S(1)} %broadcast_maximum_fusion, pred[256,4096]{1,0:T(8,128)(4,1)S(1)} %fusion.6), kind=kLoop, calls=%fused_computation.3 | loop fusion | flops 33552384 | bytes 34619392 | tf_op jit(solution)/shard_map/reduce_sum | solution.py:84
  269.4 0.6 add_select_fusion
  270.0 15.2 %fusion.16 = bf16[256,8,96]{0,2,1:T(8,128)(2,1)S(1)} fusion(bf16[4096,8,2,96]{0,3,2,1:T(8,128)(2,1)} %bitcast.70, f32[8,256,4096]{2,1,0:T(8,128)} %get-tuple-element.28, f32[8,256]{1,0:T(8,128)S(1)} %broadcast_maximum_fusion, pred[256,4096]{1,0:T(8,128)(4,1)S(1)} %fusion.6, f32[256,8]{0,1:T(8,128)S(1)} %bitcast.74, pred[256]{0:T(512)(128)(4,1)S(1)} %broadcast_compare_fusion), kind=kOutput, calls=%fused_computation.15 | convolution fusion | flops 1644756992 | bytes 41304320 | tf_op jit(solution)/shard_map/hqk,khe->hqe/dot_general | solution.py:85
  285.2 0.9 copy.39
  286.1 1.1 copy.55
  (20 shorter events, 0.7 us)
Async XLA Ops:
  7.2 13.5 %all-gather.3.cloned.1.call-start = ((), (), s32[]{:S(2)}) async-start(), calls=%async_computation.1 | async-start | bytes 2359296 | tf_op jit(solution)/shard_map/all_gather | solution.py:57
  7.9 228.9 %all-gather.5.cloned.1.call-start = ((), (), s32[]{:S(2)}) async-start(), calls=%async_computation.2 | async-start | bytes 13369344 | tf_op jit(solution)/shard_map/all_gather | solution.py:67
  29.9 1.6 copy-start
  37.1 52.6 %all-to-all-start = ((bf16[16,32,1536]{2,1,0:T(8,128)(2,1)}), bf16[16,32,1536]{2,1,0:T(8,128)(2,1)S(1)}, u32[]{:S(2)}, u32[]{:S(2)}) async-start(bf16[16,32,1536]{2,1,0:T(8,128)(2,1)} %bitcast.19), calls=%async_computation | async-start | bytes 3145728 | tf_op jit(solution)/shard_map/all_to_all | solution.py:110
Sparse Core Ops, SparseCore 0:
  9.5 11.0 all-gather.2
  31.7 205.1 all-gather.4
where the time goes:
time: 298 us; the launch traced here: 294 us
  waiting for transfers between devices  203 us (68%)
  matrix products  41.5 us (14%)
  other arithmetic  21.1 us (7%)
  between operations  14.2 us (5%)
  starting transfers between devices  7.02 us (2%)
  local copies, waits for them, and re-layouts  6.89 us (2%)
    all_gather x1, waiting for transfers between devices, body(): shard_piece = lax.all_gather(packed, 'seq', axis=0, tiled=True)  147 us
    all_to_all x1, waiting for transfers between devices, body(): lax.all_to_all(outbox.reshape(seq_count, capacity, packed.shape[1]), 'seq...  44.3 us
    dot_general x1, matrix products, body(): jnp.einsum('qhe,khe->hqk', queries, key_value[:, :, 0], preferred_element...  17.1 us
    reduce_sum x1, other arithmetic, body(): denominator = jnp.sum(weights, axis=2)  15.5 us
    dot_general x1, matrix products, body(): jnp.einsum('hqk,khe->hqe', weights.astype(jnp.bfloat16), key_value[:, :,...  15.2 us
    all_gather x1, waiting for transfers between devices, body(): lax.all_gather(stream_x, 'head', axis=1, tiled=True)  11.4 us
    dot_general x1, matrix products, body(): jnp.dot(lax.all_gather(stream_x, 'head', axis=1, tiled=True), qkv_weight,...  9.23 us
    all_to_all x1, starting transfers between devices, body(): lax.all_to_all(outbox.reshape(seq_count, capacity, packed.shape[1]), 'seq...  6.94 us
  transfers between devices with their start and end apart: 3, of which 3 were waited for; matrix products, arithmetic and copies ran while one was open for 3% of the time, Pallas kernels for 0%

commit v1 on v0

v1 whole, which is shorter than its diff:
```python
import functools
import math

import jax
import jax.numpy as jnp
from jax import lax
from jax.experimental import pallas as pl
from jax.experimental.pallas import tpu as pltpu
from jax.sharding import PartitionSpec as P

HD = 96
PART = 3 * HD
HALF = HD // 2
rope_base = 10000.0
MESH = pl.DeviceIdType.MESH
F32 = jnp.float32
BF16 = jnp.bfloat16
SCALE2 = math.log2(math.e) / math.sqrt(HD)
LN2 = math.log(2.0)
LOW = -1e30


def kernel(
    n_seq, n_head, n_long,
    page_ref, x_ref, w_ref, cos_ref, sin_ref, begin_ref, pad_ref,
    att_ref, lse_ref, kv_ref,
    wbuf, xbuf, acc, proj, qkv, rows, outbox, inbuf, krow, near, obuf, lbuf, att, lse,
    wsem, xsend, xrecv, lsend, lrecv, nsend, nrecv, csend, crecv, asend, arecv, msend, mrecv,
):
    me = lax.axis_index("seq")
    core = lax.axis_index("head")
    tok, feat = x_ref.shape
    heads = qkv.shape[0]
    _, tiles, _, width = wbuf.shape
    cap = outbox.shape[1]
    pages = rows.shape[0] - 1

    def weight_copy(r, c):
        peer = lax.rem(core + r, n_head)
        return pltpu.make_async_copy(
            w_ref.at[pl.ds(pl.multiple_of(peer * feat, 128), feat), pl.ds(c * width, width)],
            wbuf.at[r, c],
            wsem.at[r, c],
        )

    for r in range(n_head):
        for c in range(tiles):
            weight_copy(r, c).start()

    barrier = pltpu.get_barrier_semaphore()

    @pl.loop(1, n_seq)
    def _(k):
        pl.semaphore_signal(
            barrier, inc=1, device_id={"seq": lax.rem(me + k, n_seq)}, device_id_type=MESH
        )

    for r in range(1, n_head):
        pl.semaphore_signal(
            barrier, inc=1, device_id={"head": lax.rem(core + r, n_head)}, device_id_type=MESH
        )
    pl.semaphore_wait(barrier, n_seq - 1 + n_head - 1)

    def feature_copy(r):
        return pltpu.make_async_remote_copy(
            src_ref=x_ref,
            dst_ref=xbuf.at[r - 1],
            send_sem=xsend.at[r - 1],
            recv_sem=xrecv.at[r - 1],
            device_id={"head": lax.rem(core + n_head - r, n_head)},
            device_id_type=MESH,
        )

    for r in range(1, n_head):
        feature_copy(r).start()

    for r in range(n_head):
        if r > 0:
            feature_copy(r).wait_recv()

        @pl.loop(0, tiles)
        def _(c, r=r):
            weight_copy(r, 0 if tiles == 1 else c).wait()
            left = x_ref[...] if r == 0 else xbuf[r - 1]
            part = jnp.dot(left, wbuf[r, c], preferred_element_type=F32)
            if r > 0:
                part = part + acc[c]
            if r < n_head - 1:
                acc[c] = part
            else:
                proj[c] = part.T

    flat = proj.reshape(tiles * width, tok) if tiles > 1 else proj.at[0]
    cosine = cos_ref[...]
    sine = sin_ref[...]

    @pl.loop(0, heads)
    def _(h):
        base = h * PART
        for c in range(2):
            a = flat[pl.ds(pl.multiple_of(base + c * HD, 8), HALF), :]
            b = flat[pl.ds(pl.multiple_of(base + c * HD + HALF, 8), HALF), :]
            qkv[h, c * HD:c * HD + HALF, :] = (a * cosine - b * sine).astype(BF16)
            qkv[h, c * HD + HALF:(c + 1) * HD, :] = (b * cosine + a * sine).astype(BF16)
        qkv[h, 2 * HD:, :] = flat[pl.ds(pl.multiple_of(base + 2 * HD, 8), HD), :].astype(BF16)

    def long_copy(h, block):
        return pltpu.make_async_remote_copy(
            src_ref=qkv.at[h],
            dst_ref=inbuf.at[block],
            send_sem=lsend.at[h],
            recv_sem=lrecv.at[block],
            device_id={"seq": h},
            device_id_type=MESH,
        )

    @pl.when(me < n_long)
    def _():
        @pl.loop(0, heads)
        def _(h):
            @pl.when(h != me)
            def _():
                long_copy(h, me).start()

            @pl.when(h == me)
            def _():
                pltpu.make_async_copy(qkv.at[me], inbuf.at[me], lrecv.at[me]).start()

    def near_copy():
        return pltpu.make_async_remote_copy(
            src_ref=qkv.at[:, pl.ds(HD, 2 * HD)],
            dst_ref=near,
            send_sem=nsend,
            recv_sem=nrecv,
            device_id={"seq": lax.rem(me + 1, n_seq)},
            device_id_type=MESH,
        )

    sends_near = (me >= n_long - 1) & (me < n_seq - 1)

    @pl.when(sends_near)
    def _():
        near_copy().start()

    for pair in range(heads // 2):
        both = jnp.concatenate([qkv[2 * pair, HD:, :], qkv[2 * pair + 1, HD:, :]], axis=0)
        turned = both.T
        for p in range(pages):
            rows[p, :, pair * 4 * HD:(pair + 1) * 4 * HD] = turned[p * cap:(p + 1) * cap, :]
    rows[pages] = jnp.zeros(rows.shape[1:], BF16)

    def cache_copy(owner, source):
        return pltpu.make_async_remote_copy(
            src_ref=outbox.at[owner],
            dst_ref=kv_ref.at[source],
            send_sem=csend.at[owner],
            recv_sem=crecv.at[source],
            device_id={"seq": owner},
            device_id_type=MESH,
        )

    @pl.loop(0, n_seq)
    def _(o):
        outbox[o] = rows[page_ref[o]]

    own_slot = pltpu.make_async_copy(outbox.at[me], kv_ref.at[me], crecv.at[me])
    own_slot.start()

    @pl.loop(1, n_seq)
    def _(k):
        cache_copy(lax.rem(me + k, n_seq), me).start()

    query_iota = lax.broadcasted_iota(jnp.int32, (tok, tok), 1)
    key_iota = lax.broadcasted_iota(jnp.int32, (tok, tok), 0)

    def first(scores, values):
        top = jnp.max(scores, axis=0, keepdims=True)
        weights = jnp.exp2((scores - top) * SCALE2)
        total = jnp.sum(weights, axis=0, keepdims=True)
        return top, total, jnp.dot(values, weights.astype(BF16), preferred_element_type=F32)

    def more(state, scores, values):
        top, total, context = state
        new_top = jnp.maximum(top, jnp.max(scores, axis=0, keepdims=True))
        factor = jnp.exp2((top - new_top) * SCALE2)
        weights = jnp.exp2((scores - new_top) * SCALE2)
        total = factor * total + jnp.sum(weights, axis=0, keepdims=True)
        context = factor * context + jnp.dot(
            values, weights.astype(BF16), preferred_element_type=F32
        )
        return new_top, total, context

    def answer_copies(j, head):
        return [
            pltpu.make_async_remote_copy(
                src_ref=src.at[j],
                dst_ref=dst.at[head],
                send_sem=send.at[j],
                recv_sem=recv.at[head],
                device_id={"seq": j},
                device_id_type=MESH,
            )
            for src, dst, send, recv in (
                (obuf, att, asend, arecv),
                (lbuf, lse, msend, mrecv),
            )
        ]

    @pl.when(me < heads)
    def _():
        @pl.loop(0, n_long)
        def _(j):
            @pl.when(j != me)
            def _():
                long_copy(0, j).wait_recv()

            @pl.when(j == me)
            def _():
                pltpu.make_async_copy(qkv.at[me], inbuf.at[me], lrecv.at[me]).wait()

            krow[j] = inbuf[j, HD:2 * HD, :].T
            query = inbuf[j, :HD, :]

            def score(i):
                return jnp.dot(krow[i], query, preferred_element_type=F32)

            def value(i):
                return inbuf[i, 2 * HD:, :]

            state = first(jnp.where(key_iota <= query_iota, score(j), LOW), value(j))

            def two(i, state):
                scores = jnp.concatenate([score(2 * i), score(2 * i + 1)], axis=0)
                values = jnp.concatenate([value(2 * i), value(2 * i + 1)], axis=1)
                return more(state, scores, values)

            state = lax.fori_loop(0, j // 2, two, state)
            state = lax.fori_loop(
                0, lax.rem(j, 2), lambda i, s: more(s, score(j - 1), value(j - 1)), state
            )
            top, total, context = state
            obuf[j] = (context / total).astype(BF16)
            lbuf[j] = jnp.broadcast_to(top * (SCALE2 * LN2) + jnp.log(total), lbuf.shape[1:])

            @pl.when(j != me)
            def _():
                for copy in answer_copies(j, me):
                    copy.start()

            @pl.when(j == me)
            def _():
                pltpu.make_async_copy(obuf.at[me], att.at[me], arecv.at[me]).start()
                pltpu.make_async_copy(lbuf.at[me], lse.at[me], mrecv.at[me]).start()

    @pl.when(me >= n_long)
    def _():
        near_copy().wait_recv()
        begin = begin_ref[...]
        padding = pad_ref[...] > 0

        @pl.loop(0, heads)
        def _(h):
            query = qkv[h, :HD, :]
            here = jnp.dot(qkv[h, HD:2 * HD, :].T, query, preferred_element_type=F32)
            there = jnp.dot(near[h, :HD, :].T, query, preferred_element_type=F32)
            here = jnp.where((key_iota <= query_iota) & (key_iota >= begin), here, LOW)
            there = jnp.where(key_iota - tok >= begin, there, LOW)
            values = jnp.concatenate([near[h, HD:, :], qkv[h, 2 * HD:, :]], axis=1)
            top, total, context = first(jnp.concatenate([there, here], axis=0), values)
            att[h] = jnp.where(padding, 0.0, context / total).astype(BF16)
            logs = jnp.where(padding, 0.0, top * (SCALE2 * LN2) + jnp.log(total))
            lse[h] = jnp.broadcast_to(logs, lse.shape[1:])

    @pl.when(me < n_long)
    def _():
        @pl.loop(0, heads)
        def _(h):
            @pl.when(h != me)
            def _():
                for copy in answer_copies(0, h):
                    copy.wait_recv()

            @pl.when(h == me)
            def _():
                pltpu.make_async_copy(obuf.at[me], att.at[me], arecv.at[me]).wait()
                pltpu.make_async_copy(lbuf.at[me], lse.at[me], mrecv.at[me]).wait()

    for h in range(heads):
        lse_ref[h:h + 1, :] = lse[h, 0:1, :]
    att_ref[...] = att[...].reshape(heads * HD, tok).T

    for r in range(1, n_head):
        feature_copy(r).wait_send()

    @pl.when(me < n_long)
    def _():
        @pl.loop(0, heads)
        def _(h):
            @pl.when(h != me)
            def _():
                long_copy(h, me).wait_send()

    @pl.when(sends_near)
    def _():
        near_copy().wait_send()

    @pl.when(me < heads)
    def _():
        @pl.loop(0, n_long)
        def _(j):
            @pl.when(j != me)
            def _():
                for copy in answer_copies(j, me):
                    copy.wait_send()

    own_slot.wait()

    @pl.loop(1, n_seq)
    def _(k):
        other = lax.rem(me + k, n_seq)
        cache_copy(other, other).wait_recv()
        cache_copy(other, me).wait_send()


def body(n_seq, n_head, stream_x, qkv_weight, short_lengths, cache_owner):
    tok, feat = stream_x.shape
    cols = qkv_weight.shape[1]
    heads = cols // PART
    n_long = n_seq * 11 // 16
    long_length = tok * n_long
    n_short = short_lengths.shape[0]
    cap = 2 * tok // n_seq
    pages = tok // cap
    width = 256 if cols % 256 == 0 else cols
    tiles = cols // width

    first_row = lax.axis_index("seq") * tok
    order = jnp.arange(n_short + 1, dtype=jnp.int32)
    before = jnp.arange(n_short, dtype=jnp.int32)[None, :] < order[:, None]
    bounds = long_length + jnp.sum(jnp.where(before, short_lengths[None, :], 0), axis=1)
    row_ids = first_row + jnp.arange(tok, dtype=jnp.int32)
    passed = row_ids[None, :] >= bounds[:, None]
    seg_begin = jnp.max(jnp.where(passed, bounds[:, None], 0), axis=0)
    padding = passed[n_short].astype(jnp.int32)
    position = (row_ids - seg_begin).astype(F32)
    inverse_freq = rope_base ** (-jnp.arange(HALF, dtype=F32) / HALF)
    angle = inverse_freq[:, None] * position[None, :]
    page_owner = cache_owner[::cap, 0]
    match = page_owner[None, :] == jnp.arange(n_seq, dtype=jnp.int32)[:, None]
    match = match & (padding[::cap][None, :] == 0)
    page_of = pages + jnp.sum(
        jnp.where(match, jnp.arange(pages, dtype=jnp.int32)[None, :] - pages, 0), axis=1
    )

    vmem = pl.BlockSpec(memory_space=pltpu.VMEM)
    hbm = pl.BlockSpec(memory_space=pl.ANY)
    dma = pltpu.SemaphoreType.DMA
    attended, row_lse, cache = pl.pallas_call(
        functools.partial(kernel, n_seq, n_head, n_long),
        out_shape=(
            jax.ShapeDtypeStruct((tok, heads * HD), BF16),
            jax.ShapeDtypeStruct((heads, tok), F32),
            jax.ShapeDtypeStruct((n_seq, cap, heads * 2 * HD), BF16),
        ),
        in_specs=[
            pl.BlockSpec(memory_space=pltpu.SMEM), vmem, hbm, vmem, vmem, vmem, vmem,
        ],
        out_specs=(vmem, vmem, hbm),
        scratch_shapes=[
            pltpu.VMEM((n_head, tiles, feat, width), BF16),
            pltpu.VMEM((n_head - 1, tok, feat), BF16),
            pltpu.VMEM((tiles, tok, width), F32),
            pltpu.VMEM((tiles, width, tok), F32),
            pltpu.VMEM((heads, PART, tok), BF16),
            pltpu.VMEM((pages + 1, cap, heads * 2 * HD), BF16),
            pltpu.VMEM((n_seq, cap, heads * 2 * HD), BF16),
            pltpu.VMEM((n_long, PART, tok), BF16),
            pltpu.VMEM((n_long, tok, HD), BF16),
            pltpu.VMEM((heads, 2 * HD, tok), BF16),
            pltpu.VMEM((n_long, HD, tok), BF16),
            pltpu.VMEM((n_long, 8, tok), F32),
            pltpu.VMEM((heads, HD, tok), BF16),
            pltpu.VMEM((heads, 8, tok), F32),
            dma((n_head, tiles)),
            dma((n_head - 1,)),
            dma((n_head - 1,)),
            dma((heads,)),
            dma((n_long,)),
            dma,
            dma,
            dma((n_seq,)),
            dma((n_seq,)),
            dma((n_long,)),
            dma((heads,)),
            dma((n_long,)),
            dma((heads,)),
        ],
        compiler_params=pltpu.CompilerParams(
            collective_id=0, has_side_effects=True, vmem_limit_bytes=50 * 1024 * 1024
        ),
        cost_estimate=pl.CostEstimate(
            flops=2 * tok * feat * n_head * cols, bytes_accessed=2 * feat * n_head * cols,
            transcendentals=0,
        ),
    )(
        page_of, stream_x, qkv_weight, jnp.cos(angle), jnp.sin(angle),
        (seg_begin - first_row)[None, :], padding[None, :],
    )
    return attended, row_lse, cache.reshape(n_seq * cap, heads * 2 * HD)


def solution(mesh):
    return jax.shard_map(
        functools.partial(body, mesh.shape["seq"], mesh.shape["head"]),
        mesh=mesh,
        in_specs=(P("seq", "head"), P(None, "head"), P(), P("seq", None)),
        out_specs=(P("seq", "head"), P("head", "seq"), P("seq", "head")),
        check_vma=False,
    )
```

time: 298 us -> 82.9 us (0.28)
  the two profiles are of different devices: /device:TPU:20 before, /device:TPU:6 now
where the time goes in v1:
time: 82.9 us; the launch traced here: 82.7 us
  Pallas kernels  76.2 us (92%)
  local copies, waits for them, and re-layouts  4.48 us (5%)
  other arithmetic  1.32 us (2%)
    pallas_call x1, Pallas kernels, body(): pl.pallas_call(functools.partial(kernel, n_seq, n_head, n_long), out_shap...  76.2 us
    unnamed x5, local copies, waits for them, and re-layouts  3.62 us

profile of v1, /device:TPU:6, one launch (start us, length us, event | category | flops | bytes accessed | tf_op | source)
XLA Modules:
  0.0 82.7 jit_solution(11568182280849403972)
XLA Ops:
  0.6 0.7 select_reduce_fusion.2
  1.4 0.8 slice.12
  2.2 0.1 select_reduce_fusion
  2.3 0.1 broadcast_compare_fusion
  2.4 0.1 slice.14
  2.5 0.1 select_reduce_fusion.1
  2.6 0.3 multiply_sine_fusion
  2.8 0.0 copy-start
  2.9 1.1 %copy-done = bf16[256,1536]{1,0:T(8,128)(2,1)S(1)} copy-done((bf16[256,1536]{1,0:T(8,128)(2,1)S(1)}, bf16[256,1536]{1,0:T(8,128)(2,1)}, u32[]{:S(2)}) %copy-start) | copy-done | bytes 786456
  4.0 76.2 %shard_map.67 = (bf16[256,768]{1,0:T(8,128)(2,1)S(1)}, f32[8,256]{1,0:T(8,128)S(1)}, bf16[16,32,1536]{2,1,0:T(8,128)(2,1)S(1)}) custom-call(s32[16]{0:T(128)S(1)} %broadcast_add_fusion.page_ref, bf16[256,1536]{1,0:T(8,128)(2,1)S(1)} %copy-done, bf16[3072,2304]{1,0:T(8,128)(2,1)} %w_ref.1, f32[48,256]{1,0:T(8,128)S(1)} %get-tuple-element.12.cos_ref, ...), custom_call_target="tpu_custom_call" | custom-call | flops 3623878656 | bytes 14155776 | tf_op jit(solution)/shard_map/pallas_call | solution.py:358
  80.2 0.7 copy.10
  81.0 0.6 copy.11
  81.6 1.1 %copy.12 = bf16[512,1536]{1,0:T(8,128)(2,1)} copy(bf16[512,1536]{1,0:T(8,128)(2,1)S(1)} %bitcast.3) | data formatting | bytes 3145728
  (8 shorter events, 0.1 us)
Async XLA Ops:
  2.8 1.1 %copy-start = (bf16[256,1536]{1,0:T(8,128)(2,1)S(1)}, bf16[256,1536]{1,0:T(8,128)(2,1)}, u32[]{:S(2)}) copy-start(bf16[256,1536]{1,0:T(8,128)(2,1)} %x_ref.1) | copy-start | bytes 2359300

commit v2 on v1

--- a/solution.py
+++ b/solution.py
@@ -34,6 +34,8 @@
     _, tiles, _, width = wbuf.shape
     cap = outbox.shape[1]
     pages = rows.shape[0] - 1
+    n_real = n_long + n_seq // 4
+    burst = pl.cdiv(n_seq - 1, n_long)
 
     def weight_copy(r, c):
         peer = lax.rem(core + r, n_head)
@@ -117,7 +119,9 @@
     @pl.when(me < n_long)
     def _():
         @pl.loop(0, heads)
-        def _(h):
+        def _(k):
+            h = lax.rem(me + 1 + k, heads)
+
             @pl.when(h != me)
             def _():
                 long_copy(h, me).start()
@@ -163,12 +167,32 @@
     def _(o):
         outbox[o] = rows[page_ref[o]]
 
-    own_slot = pltpu.make_async_copy(outbox.at[me], kv_ref.at[me], crecv.at[me])
-    own_slot.start()
-
-    @pl.loop(1, n_seq)
-    def _(k):
-        cache_copy(lax.rem(me + k, n_seq), me).start()
+    def own_slot():
+        return pltpu.make_async_copy(outbox.at[me], kv_ref.at[me], crecv.at[me])
+
+    def zero_slot(s):
+        return pltpu.make_async_copy(rows.at[pages], kv_ref.at[s], crecv.at[s])
+
+    @pl.when(me < n_real)
+    def _():
+        own_slot().start()
+
+    @pl.loop(n_real, n_seq)
+    def _(s):
+        zero_slot(s).start()
+
+    def send_cache(first_step, last_step):
+        @pl.loop(first_step, last_step)
+        def _(k):
+            cache_copy(lax.rem(me + k, n_seq), me).start()
+
+    @pl.when((me >= heads) & (me < n_long))
+    def _():
+        @pl.loop(0, heads)
+        def _(h):
+            long_copy(h, me).wait_send()
+
+        send_cache(1, n_seq)
 
     query_iota = lax.broadcasted_iota(jnp.int32, (tok, tok), 1)
     key_iota = lax.broadcasted_iota(jnp.int32, (tok, tok), 0)
@@ -218,6 +242,9 @@
             def _():
                 pltpu.make_async_copy(qkv.at[me], inbuf.at[me], lrecv.at[me]).wait()
 
+            send_cache(
+                jnp.minimum(1 + j * burst, n_seq), jnp.minimum(1 + (j + 1) * burst, n_seq)
+            )
             krow[j] = inbuf[j, HD:2 * HD, :].T
             query = inbuf[j, :HD, :]
 
@@ -229,15 +256,19 @@
 
             state = first(jnp.where(key_iota <= query_iota, score(j), LOW), value(j))
 
-            def two(i, state):
-                scores = jnp.concatenate([score(2 * i), score(2 * i + 1)], axis=0)
-                values = jnp.concatenate([value(2 * i), value(2 * i + 1)], axis=1)
-                return more(state, scores, values)
-
-            state = lax.fori_loop(0, j // 2, two, state)
-            state = lax.fori_loop(
-                0, lax.rem(j, 2), lambda i, s: more(s, score(j - 1), value(j - 1)), state
-            )
+            def several(count, start):
+                def step(i, state):
+                    blocks = [start + i * count + b for b in range(count)]
+                    scores = jnp.concatenate([score(b) for b in blocks], axis=0)
+                    values = jnp.concatenate([value(b) for b in blocks], axis=1)
+                    return more(state, scores, values)
+
+                return step
+
+            state = lax.fori_loop(0, j // 4, several(4, 0), state)
+            left = lax.rem(j, 4)
+            state = lax.fori_loop(0, left // 2, several(2, j - left), state)
+            state = lax.fori_loop(0, lax.rem(j, 2), several(1, j - 1), state)
             top, total, context = state
             obuf[j] = (context / total).astype(BF16)
             lbuf[j] = jnp.broadcast_to(top * (SCALE2 * LN2) + jnp.log(total), lbuf.shape[1:])
@@ -271,6 +302,10 @@
             logs = jnp.where(padding, 0.0, top * (SCALE2 * LN2) + jnp.log(total))
             lse[h] = jnp.broadcast_to(logs, lse.shape[1:])
 
+        @pl.when(me < n_real)
+        def _():
+            send_cache(1, n_seq)
+
     @pl.when(me < n_long)
     def _():
         @pl.loop(0, heads)
@@ -292,7 +327,7 @@
     for r in range(1, n_head):
         feature_copy(r).wait_send()
 
-    @pl.when(me < n_long)
+    @pl.when(me < heads)
     def _():
         @pl.loop(0, heads)
         def _(h):
@@ -313,13 +348,23 @@
                 for copy in answer_copies(j, me):
                     copy.wait_send()
 
-    own_slot.wait()
-
-    @pl.loop(1, n_seq)
-    def _(k):
-        other = lax.rem(me + k, n_seq)
-        cache_copy(other, other).wait_recv()
-        cache_copy(other, me).wait_send()
+    @pl.when(me < n_real)
+    def _():
+        own_slot().wait()
+
+        @pl.loop(1, n_seq)
+        def _(k):
+            cache_copy(lax.rem(me + k, n_seq), me).wait_send()
+
+    @pl.loop(0, n_real)
+    def _(s):
+        @pl.when(s != me)
+        def _():
+            cache_copy(s, s).wait_recv()
+
+    @pl.loop(n_real, n_seq)
+    def _(s):
+        zero_slot(s).wait()
 
 
 def body(n_seq, n_head, stream_x, qkv_weight, short_lengths, cache_owner):

time: 82.9 us -> 84.8 us (1.023)
  the two profiles are of different devices: /device:TPU:6 before, /device:TPU:14 now
where the time goes in v2:
time: 84.8 us; the launch traced here: 84.6 us
  Pallas kernels  78.1 us (92%)
  local copies, waits for them, and re-layouts  4.48 us (5%)
  other arithmetic  1.32 us (2%)
    pallas_call x1, Pallas kernels, body(): pl.pallas_call(functools.partial(kernel, n_seq, n_head, n_long), out_shap...  78.1 us
    unnamed x5, local copies, waits for them, and re-layouts  3.62 us

profile of v2, /device:TPU:14, one launch (start us, length us, event | category | flops | bytes accessed | tf_op | source)
XLA Modules:
  0.0 84.6 jit_solution(8919691034993064737)
XLA Ops:
  0.6 0.7 select_reduce_fusion.2
  1.4 0.8 slice.12
  2.2 0.1 select_reduce_fusion
  2.3 0.1 broadcast_compare_fusion
  2.4 0.1 slice.14
  2.5 0.1 select_reduce_fusion.1
  2.6 0.3 multiply_sine_fusion
  2.8 0.0 copy-start
  2.9 1.1 %copy-done = bf16[256,1536]{1,0:T(8,128)(2,1)S(1)} copy-done((bf16[256,1536]{1,0:T(8,128)(2,1)S(1)}, bf16[256,1536]{1,0:T(8,128)(2,1)}, u32[]{:S(2)}) %copy-start) | copy-done | bytes 786456
  4.0 78.1 %shard_map.67 = (bf16[256,768]{1,0:T(8,128)(2,1)S(1)}, f32[8,256]{1,0:T(8,128)S(1)}, bf16[16,32,1536]{2,1,0:T(8,128)(2,1)S(1)}) custom-call(s32[16]{0:T(128)S(1)} %broadcast_add_fusion.page_ref, bf16[256,1536]{1,0:T(8,128)(2,1)S(1)} %copy-done, bf16[3072,2304]{1,0:T(8,128)(2,1)} %w_ref.1, f32[48,256]{1,0:T(8,128)S(1)} %get-tuple-element.12.cos_ref, ...), custom_call_target="tpu_custom_call" | custom-call | flops 3623878656 | bytes 14155776 | tf_op jit(solution)/shard_map/pallas_call | solution.py:403
  82.1 0.7 copy.10
  82.8 0.6 copy.11
  83.4 1.1 %copy.12 = bf16[512,1536]{1,0:T(8,128)(2,1)} copy(bf16[512,1536]{1,0:T(8,128)(2,1)S(1)} %bitcast.3) | data formatting | bytes 3145728
  (8 shorter events, 0.1 us)
Async XLA Ops:
  2.8 1.1 %copy-start = (bf16[256,1536]{1,0:T(8,128)(2,1)S(1)}, bf16[256,1536]{1,0:T(8,128)(2,1)}, u32[]{:S(2)}) copy-start(bf16[256,1536]{1,0:T(8,128)(2,1)} %x_ref.1) | copy-start | bytes 2359300

commit v3 on v2

--- a/solution.py
+++ b/solution.py
@@ -3,6 +3,7 @@
 
 import jax
 import jax.numpy as jnp
+import numpy as np
 from jax import lax
 from jax.experimental import pallas as pl
 from jax.experimental.pallas import tpu as pltpu
@@ -20,36 +21,59 @@
 LOW = -1e30
 
 
+def circular(angle):
+    turns = jnp.floor(angle * (2.0 / math.pi) + 0.5)
+    rest = angle - turns * 1.5703125
+    rest = rest - turns * 4.837512969970703125e-4
+    rest = rest - turns * 7.54978995489188216e-8
+    z = rest * rest
+    sine = ((-1.9515295891e-4 * z + 8.3321608736e-3) * z - 1.6666654611e-1) * z * rest + rest
+    cosine = (
+        ((2.443315711809948e-5 * z - 1.388731625493765e-3) * z + 4.166664568298827e-2) * z * z
+        - 0.5 * z
+        + 1.0
+    )
+    quarter = turns - 4.0 * jnp.floor(turns * 0.25)
+    odd = (quarter == 1.0) | (quarter == 3.0)
+    cos_low = (quarter == 1.0) | (quarter == 2.0)
+    sin_low = quarter >= 2.0
+    cos_size = jnp.where(odd, sine, cosine)
+    sin_size = jnp.where(odd, cosine, sine)
+    return jnp.where(cos_low, -cos_size, cos_size), jnp.where(sin_low, -sin_size, sin_size)
+
+
 def kernel(
     n_seq, n_head, n_long,
-    page_ref, x_ref, w_ref, cos_ref, sin_ref, begin_ref, pad_ref,
+    short_ref, owner_ref, freq_ref, x_ref, w_ref,
     att_ref, lse_ref, kv_ref,
-    wbuf, xbuf, acc, proj, qkv, rows, outbox, inbuf, krow, near, obuf, lbuf, att, lse,
-    wsem, xsend, xrecv, lsend, lrecv, nsend, nrecv, csend, crecv, asend, arecv, msend, mrecv,
+    wbuf, xbuf, proj, cosine, sine, qkv, rows, outbox, inbuf, krow, near, obuf, lbuf,
+    wsem, xown, xsend, xrecv, lsend, lrecv, nsend, nrecv, csend, crecv, asend, arecv, msend, mrecv,
 ):
     me = lax.axis_index("seq")
     core = lax.axis_index("head")
     tok, feat = x_ref.shape
     heads = qkv.shape[0]
-    _, tiles, _, width = wbuf.shape
+    tiles, _, width = wbuf.shape
     cap = outbox.shape[1]
     pages = rows.shape[0] - 1
     n_real = n_long + n_seq // 4
-    burst = pl.cdiv(n_seq - 1, n_long)
-
-    def weight_copy(r, c):
-        peer = lax.rem(core + r, n_head)
+
+    def weight_copy(c):
         return pltpu.make_async_copy(
-            w_ref.at[pl.ds(pl.multiple_of(peer * feat, 128), feat), pl.ds(c * width, width)],
-            wbuf.at[r, c],
-            wsem.at[r, c],
-        )
-
-    for r in range(n_head):
-        for c in range(tiles):
-            weight_copy(r, c).start()
+            w_ref.at[:, pl.ds(c * width, width)], wbuf.at[c], wsem.at[c]
+        )
+
+    own_features = pltpu.make_async_copy(x_ref, xbuf.at[core], xown)
+    own_features.start()
+    for c in range(tiles):
+        weight_copy(c).start()
 
     barrier = pltpu.get_barrier_semaphore()
+
+    for r in range(1, n_head):
+        pl.semaphore_signal(
+            barrier, inc=1, device_id={"head": lax.rem(core + r, n_head)}, device_id_type=MESH
+        )
 
     @pl.loop(1, n_seq)
     def _(k):
@@ -57,54 +81,49 @@
             barrier, inc=1, device_id={"seq": lax.rem(me + k, n_seq)}, device_id_type=MESH
         )
 
-    for r in range(1, n_head):
-        pl.semaphore_signal(
-            barrier, inc=1, device_id={"head": lax.rem(core + r, n_head)}, device_id_type=MESH
-        )
+    first_row = me * tok
+    row_ids = first_row + lax.broadcasted_iota(jnp.int32, (1, tok), 1)
+    bound = n_long * tok
+    begin = jnp.zeros((1, tok), jnp.int32)
+    for j in range(short_ref.shape[0] + 1):
+        begin = jnp.where(row_ids >= bound, bound, begin)
+        padding = row_ids >= bound
+        if j < short_ref.shape[0]:
+            bound = bound + short_ref[j]
+    angle = freq_ref[...] * (row_ids - begin).astype(F32)
+    begin = begin - first_row
+    cos_value, sin_value = circular(angle)
+    cosine[...] = cos_value
+    sine[...] = sin_value
+
     pl.semaphore_wait(barrier, n_seq - 1 + n_head - 1)
 
     def feature_copy(r):
         return pltpu.make_async_remote_copy(
             src_ref=x_ref,
-            dst_ref=xbuf.at[r - 1],
+            dst_ref=xbuf.at[core],
             send_sem=xsend.at[r - 1],
             recv_sem=xrecv.at[r - 1],
             device_id={"head": lax.rem(core + n_head - r, n_head)},
             device_id_type=MESH,
         )
 
+    def feature_arrival(r):
+        peer = lax.rem(core + r, n_head)
+        return pltpu.make_async_remote_copy(
+            src_ref=x_ref,
+            dst_ref=xbuf.at[peer],
+            send_sem=xsend.at[r - 1],
+            recv_sem=xrecv.at[r - 1],
+            device_id={"head": peer},
+            device_id_type=MESH,
+        )
+
     for r in range(1, n_head):
         feature_copy(r).start()
-
-    for r in range(n_head):
-        if r > 0:
-            feature_copy(r).wait_recv()
-
-        @pl.loop(0, tiles)
-        def _(c, r=r):
-            weight_copy(r, 0 if tiles == 1 else c).wait()
-            left = x_ref[...] if r == 0 else xbuf[r - 1]
-            part = jnp.dot(left, wbuf[r, c], preferred_element_type=F32)
-            if r > 0:
-                part = part + acc[c]
-            if r < n_head - 1:
-                acc[c] = part
-            else:
-                proj[c] = part.T
-
-    flat = proj.reshape(tiles * width, tok) if tiles > 1 else proj.at[0]
-    cosine = cos_ref[...]
-    sine = sin_ref[...]
-
-    @pl.loop(0, heads)
-    def _(h):
-        base = h * PART
-        for c in range(2):
-            a = flat[pl.ds(pl.multiple_of(base + c * HD, 8), HALF), :]
-            b = flat[pl.ds(pl.multiple_of(base + c * HD + HALF, 8), HALF), :]
-            qkv[h, c * HD:c * HD + HALF, :] = (a * cosine - b * sine).astype(BF16)
-            qkv[h, c * HD + HALF:(c + 1) * HD, :] = (b * cosine + a * sine).astype(BF16)
-        qkv[h, 2 * HD:, :] = flat[pl.ds(pl.multiple_of(base + 2 * HD, 8), HD), :].astype(BF16)
+    own_features.wait()
+    for r in range(1, n_head):
+        feature_arrival(r).wait_recv()
 
     def long_copy(h, block):
         return pltpu.make_async_remote_copy(
@@ -116,13 +135,30 @@
             device_id_type=MESH,
         )
 
-    @pl.when(me < n_long)
-    def _():
-        @pl.loop(0, heads)
-        def _(k):
-            h = lax.rem(me + 1 + k, heads)
-
-            @pl.when(h != me)
+    @pl.loop(0, tiles)
+    def _(c):
+        weight_copy(c).wait()
+        part = jnp.zeros((tok, width), F32)
+        for r in range(n_head):
+            part = part + jnp.dot(
+                xbuf[r], wbuf[c, r * feat:(r + 1) * feat, :], preferred_element_type=F32
+            )
+        proj[pl.ds(pl.multiple_of(c * width, 8), width), :] = part.T
+
+        @pl.loop(c * width // PART, (c + 1) * width // PART)
+        def _(h):
+            base = h * PART
+            for part_id in range(2):
+                low = part_id * HD
+                a = proj[pl.ds(pl.multiple_of(base + low, 8), HALF), :]
+                b = proj[pl.ds(pl.multiple_of(base + low + HALF, 8), HALF), :]
+                qkv[h, low:low + HALF, :] = (a * cosine[...] - b * sine[...]).astype(BF16)
+                qkv[h, low + HALF:low + HD, :] = (b * cosine[...] + a * sine[...]).astype(BF16)
+            qkv[h, 2 * HD:, :] = proj[
+                pl.ds(pl.multiple_of(base + 2 * HD, 8), HD), :
+            ].astype(BF16)
+
+            @pl.when((me < n_long) & (h != me))
             def _():
                 long_copy(h, me).start()
 
@@ -165,7 +201,10 @@
 
     @pl.loop(0, n_seq)
     def _(o):
-        outbox[o] = rows[page_ref[o]]
+        page = pages
+        for p in range(pages):
+            page = jnp.where(owner_ref[p * cap] == o, p, page)
+        outbox[o] = rows[page]
 
     def own_slot():
         return pltpu.make_async_copy(outbox.at[me], kv_ref.at[me], crecv.at[me])
@@ -181,18 +220,11 @@
     def _(s):
         zero_slot(s).start()
 
-    def send_cache(first_step, last_step):
-        @pl.loop(first_step, last_step)
+    @pl.when(me < n_real)
+    def _():
+        @pl.loop(1, n_seq)
         def _(k):
             cache_copy(lax.rem(me + k, n_seq), me).start()
-
-    @pl.when((me >= heads) & (me < n_long))
-    def _():
-        @pl.loop(0, heads)
-        def _(h):
-            long_copy(h, me).wait_send()
-
-        send_cache(1, n_seq)
 
     query_iota = lax.broadcasted_iota(jnp.int32, (tok, tok), 1)
     key_iota = lax.broadcasted_iota(jnp.int32, (tok, tok), 0)
@@ -225,8 +257,8 @@
                 device_id_type=MESH,
             )
             for src, dst, send, recv in (
-                (obuf, att, asend, arecv),
-                (lbuf, lse, msend, mrecv),
+                (obuf, att_ref, asend, arecv),
+                (lbuf, lse_ref, msend, mrecv),
             )
         ]
 
@@ -242,9 +274,6 @@
             def _():
                 pltpu.make_async_copy(qkv.at[me], inbuf.at[me], lrecv.at[me]).wait()
 
-            send_cache(
-                jnp.minimum(1 + j * burst, n_seq), jnp.minimum(1 + (j + 1) * burst, n_seq)
-            )
             krow[j] = inbuf[j, HD:2 * HD, :].T
             query = inbuf[j, :HD, :]
 
@@ -280,14 +309,12 @@
 
             @pl.when(j == me)
             def _():
-                pltpu.make_async_copy(obuf.at[me], att.at[me], arecv.at[me]).start()
-                pltpu.make_async_copy(lbuf.at[me], lse.at[me], mrecv.at[me]).start()
+                pltpu.make_async_copy(obuf.at[me], att_ref.at[me], arecv.at[me]).start()
+                pltpu.make_async_copy(lbuf.at[me], lse_ref.at[me], mrecv.at[me]).start()
 
     @pl.when(me >= n_long)
     def _():
         near_copy().wait_recv()
-        begin = begin_ref[...]
-        padding = pad_ref[...] > 0
 
         @pl.loop(0, heads)
         def _(h):
@@ -298,13 +325,9 @@
             there = jnp.where(key_iota - tok >= begin, there, LOW)
             values = jnp.concatenate([near[h, HD:, :], qkv[h, 2 * HD:, :]], axis=1)
             top, total, context = first(jnp.concatenate([there, here], axis=0), values)
-            att[h] = jnp.where(padding, 0.0, context / total).astype(BF16)
+            att_ref[h] = jnp.where(padding, 0.0, context / total).astype(BF16)
             logs = jnp.where(padding, 0.0, top * (SCALE2 * LN2) + jnp.log(total))
-            lse[h] = jnp.broadcast_to(logs, lse.shape[1:])
-
-        @pl.when(me < n_real)
-        def _():
-            send_cache(1, n_seq)
+            lse_ref[h] = jnp.broadcast_to(logs, lse_ref.shape[1:])
 
     @pl.when(me < n_long)
     def _():
@@ -317,17 +340,13 @@
 
             @pl.when(h == me)
             def _():
-                pltpu.make_async_copy(obuf.at[me], att.at[me], arecv.at[me]).wait()
-                pltpu.make_async_copy(lbuf.at[me], lse.at[me], mrecv.at[me]).wait()
-
-    for h in range(heads):
-        lse_ref[h:h + 1, :] = lse[h, 0:1, :]
-    att_ref[...] = att[...].reshape(heads * HD, tok).T
+                pltpu.make_async_copy(obuf.at[me], att_ref.at[me], arecv.at[me]).wait()
+                pltpu.make_async_copy(lbuf.at[me], lse_ref.at[me], mrecv.at[me]).wait()
 
     for r in range(1, n_head):
         feature_copy(r).wait_send()
 
-    @pl.when(me < heads)
+    @pl.when(me < n_long)
     def _():
         @pl.loop(0, heads)
         def _(h):
@@ -372,50 +391,31 @@
     cols = qkv_weight.shape[1]
     heads = cols // PART
     n_long = n_seq * 11 // 16
-    long_length = tok * n_long
-    n_short = short_lengths.shape[0]
     cap = 2 * tok // n_seq
     pages = tok // cap
     width = 256 if cols % 256 == 0 else cols
     tiles = cols // width
 
-    first_row = lax.axis_index("seq") * tok
-    order = jnp.arange(n_short + 1, dtype=jnp.int32)
-    before = jnp.arange(n_short, dtype=jnp.int32)[None, :] < order[:, None]
-    bounds = long_length + jnp.sum(jnp.where(before, short_lengths[None, :], 0), axis=1)
-    row_ids = first_row + jnp.arange(tok, dtype=jnp.int32)
-    passed = row_ids[None, :] >= bounds[:, None]
-    seg_begin = jnp.max(jnp.where(passed, bounds[:, None], 0), axis=0)
-    padding = passed[n_short].astype(jnp.int32)
-    position = (row_ids - seg_begin).astype(F32)
-    inverse_freq = rope_base ** (-jnp.arange(HALF, dtype=F32) / HALF)
-    angle = inverse_freq[:, None] * position[None, :]
-    page_owner = cache_owner[::cap, 0]
-    match = page_owner[None, :] == jnp.arange(n_seq, dtype=jnp.int32)[:, None]
-    match = match & (padding[::cap][None, :] == 0)
-    page_of = pages + jnp.sum(
-        jnp.where(match, jnp.arange(pages, dtype=jnp.int32)[None, :] - pages, 0), axis=1
-    )
-
+    inverse_freq = (rope_base ** (-np.arange(HALF) / HALF)).astype(np.float32)[:, None]
+    smem = pl.BlockSpec(memory_space=pltpu.SMEM)
     vmem = pl.BlockSpec(memory_space=pltpu.VMEM)
     hbm = pl.BlockSpec(memory_space=pl.ANY)
     dma = pltpu.SemaphoreType.DMA
     attended, row_lse, cache = pl.pallas_call(
         functools.partial(kernel, n_seq, n_head, n_long),
         out_shape=(
-            jax.ShapeDtypeStruct((tok, heads * HD), BF16),
-            jax.ShapeDtypeStruct((heads, tok), F32),
+            jax.ShapeDtypeStruct((heads, HD, tok), BF16),
+            jax.ShapeDtypeStruct((heads, 8, tok), F32),
             jax.ShapeDtypeStruct((n_seq, cap, heads * 2 * HD), BF16),
         ),
-        in_specs=[
-            pl.BlockSpec(memory_space=pltpu.SMEM), vmem, hbm, vmem, vmem, vmem, vmem,
-        ],
+        in_specs=[smem, smem, vmem, hbm, hbm],
         out_specs=(vmem, vmem, hbm),
         scratch_shapes=[
-            pltpu.VMEM((n_head, tiles, feat, width), BF16),
-            pltpu.VMEM((n_head - 1, tok, feat), BF16),
-            pltpu.VMEM((tiles, tok, width), F32),
-            pltpu.VMEM((tiles, width, tok), F32),
+            pltpu.VMEM((tiles, n_head * feat, width), BF16),
+            pltpu.VMEM((n_head, tok, feat), BF16),
+            pltpu.VMEM((cols, tok), F32),
+            pltpu.VMEM((HALF, tok), F32),
+            pltpu.VMEM((HALF, tok), F32),
             pltpu.VMEM((heads, PART, tok), BF16),
             pltpu.VMEM((pages + 1, cap, heads * 2 * HD), BF16),
             pltpu.VMEM((n_seq, cap, heads * 2 * HD), BF16),
@@ -424,9 +424,8 @@
             pltpu.VMEM((heads, 2 * HD, tok), BF16),
             pltpu.VMEM((n_long, HD, tok), BF16),
             pltpu.VMEM((n_long, 8, tok), F32),
-            pltpu.VMEM((heads, HD, tok), BF16),
-            pltpu.VMEM((heads, 8, tok), F32),
-            dma((n_head, tiles)),
+            dma((tiles,)),
+            dma,
             dma((n_head - 1,)),
             dma((n_head - 1,)),
             dma((heads,)),
@@ -441,17 +440,17 @@
             dma((heads,)),
         ],
         compiler_params=pltpu.CompilerParams(
-            collective_id=0, has_side_effects=True, vmem_limit_bytes=50 * 1024 * 1024
+            collective_id=0, has_side_effects=True, vmem_limit_bytes=60 * 1024 * 1024
         ),
         cost_estimate=pl.CostEstimate(
             flops=2 * tok * feat * n_head * cols, bytes_accessed=2 * feat * n_head * cols,
             transcendentals=0,
         ),
     )(
-        page_of, stream_x, qkv_weight, jnp.cos(angle), jnp.sin(angle),
-        (seg_begin - first_row)[None, :], padding[None, :],
+        short_lengths, cache_owner.reshape(tok), jnp.asarray(inverse_freq), stream_x, qkv_weight,
     )
-    return attended, row_lse, cache.reshape(n_seq * cap, heads * 2 * HD)
+    attended = attended.reshape(heads * HD, tok).T
+    return attended, row_lse[:, 0, :], cache.reshape(n_seq * cap, heads * 2 * HD)
 
 
 def solution(mesh):

time: 84.8 us -> 83.9 us (0.989)
  the two profiles are of different devices: /device:TPU:14 before, /device:TPU:15 now
where the time goes in v3:
time: 83.9 us; the launch traced here: 83.6 us
  Pallas kernels  77 us (92%)
  local copies, waits for them, and re-layouts  6.01 us (7%)
    pallas_call x1, Pallas kernels, body(): pl.pallas_call(functools.partial(kernel, n_seq, n_head, n_long), out_shap...  77 us
    unnamed x2, local copies, waits for them, and re-layouts  3.25 us
    reshape x1, local copies, waits for them, and re-layouts, body(): attended = attended.reshape(heads * HD, tok).T  1.92 us

profile of v3, /device:TPU:15, one launch (start us, length us, event | category | flops | bytes accessed | tf_op | source)
XLA Modules:
  0.0 83.6 jit_solution(8233236489130903827)
XLA Ops:
  0.6 77.0 %shard_map.76 = (bf16[8,96,256]{2,1,0:T(8,128)(2,1)}, f32[8,8,256]{2,1,0:T(8,128)}, bf16[16,32,1536]{2,1,0:T(8,128)(2,1)}) custom-call(s32[8]{0:T(128)} %short_ref.1, s32[256]{0:T(256)} %bitcast.11, f32[48,1]{1,0:T(8,128)} %constant.2.clone.freq_ref, bf16[256,1536]{1,0:T(8,128)(2,1)} %x_ref.1, bf16[3072,2304]{1,0:T(8,128)(2,1)} %w_ref.1), custom_call_target="tpu_custom_call" | custom-call | flops 3623878656 | bytes 14155776 | tf_op jit(solution)/shard_map/pallas_call | solution.py:404
  77.6 1.9 %copy.8 = bf16[768,256]{0,1:T(8,128)(2,1)} copy(bf16[768,256]{1,0:T(8,128)(2,1)} %bitcast.9) | data formatting | bytes 786432 | tf_op jit(solution)/shard_map/reshape | solution.py:452
  79.5 0.8 %slice.3 = f32[8,1,256]{2,1,0:T(1,128)S(1)} slice(f32[8,8,256]{2,1,0:T(8,128)} %get-tuple-element.7), slice={[0:8], [0:1], [0:256]} | slice | bytes 16384 | tf_op jit(solution)/shard_map/slice | solution.py:453
  80.4 0.6 copy.11
  81.0 2.7 %copy.13 = bf16[512,1536]{1,0:T(8,128)(2,1)} copy(bf16[512,1536]{1,0:T(8,128)(2,1)} %bitcast.7) | data formatting | bytes 3145728

commit v4 on v3

--- a/solution.py
+++ b/solution.py
@@ -16,8 +16,7 @@
 MESH = pl.DeviceIdType.MESH
 F32 = jnp.float32
 BF16 = jnp.bfloat16
-SCALE2 = math.log2(math.e) / math.sqrt(HD)
-LN2 = math.log(2.0)
+SCALE = 1.0 / math.sqrt(HD)
 LOW = -1e30
 
 
@@ -46,7 +45,7 @@
     n_seq, n_head, n_long,
     short_ref, owner_ref, freq_ref, x_ref, w_ref,
     att_ref, lse_ref, kv_ref,
-    wbuf, xbuf, proj, cosine, sine, qkv, rows, outbox, inbuf, krow, near, obuf, lbuf,
+    wbuf, xbuf, proj, cosine, sine, qkv, rows, outbox, inbuf, late, krow, near, obuf, lbuf, local, logged,
     wsem, xown, xsend, xrecv, lsend, lrecv, nsend, nrecv, csend, crecv, asend, arecv, msend, mrecv,
 ):
     me = lax.axis_index("seq")
@@ -57,6 +56,7 @@
     cap = outbox.shape[1]
     pages = rows.shape[0] - 1
     n_real = n_long + n_seq // 4
+    n_early = inbuf.shape[0]
 
     def weight_copy(c):
         return pltpu.make_async_copy(
@@ -135,6 +135,19 @@
             device_id_type=MESH,
         )
 
+    def query_copy(h, block):
+        return pltpu.make_async_remote_copy(
+            src_ref=qkv.at[h, pl.ds(0, HD)],
+            dst_ref=late.at[block - n_early],
+            send_sem=lsend.at[h],
+            recv_sem=lrecv.at[block],
+            device_id={"seq": h},
+            device_id_type=MESH,
+        )
+
+    is_late = (me >= n_early) & (me < n_long)
+    is_short = (me >= n_long) & (me < n_real)
+
     @pl.loop(0, tiles)
     def _(c):
         weight_copy(c).wait()
@@ -158,29 +171,39 @@
                 pl.ds(pl.multiple_of(base + 2 * HD, 8), HD), :
             ].astype(BF16)
 
-            @pl.when((me < n_long) & (h != me))
+            @pl.when((me < n_early) & (h != me))
             def _():
                 long_copy(h, me).start()
 
+            @pl.when(is_late)
+            def _():
+                query_copy(h, me).start()
+
             @pl.when(h == me)
             def _():
                 pltpu.make_async_copy(qkv.at[me], inbuf.at[me], lrecv.at[me]).start()
 
-    def near_copy():
+    def near_copy(target, slot, send_slot):
         return pltpu.make_async_remote_copy(
             src_ref=qkv.at[:, pl.ds(HD, 2 * HD)],
-            dst_ref=near,
-            send_sem=nsend,
-            recv_sem=nrecv,
-            device_id={"seq": lax.rem(me + 1, n_seq)},
+            dst_ref=near.at[slot],
+            send_sem=nsend.at[send_slot],
+            recv_sem=nrecv.at[slot],
+            device_id={"seq": target},
             device_id_type=MESH,
         )
 
-    sends_near = (me >= n_long - 1) & (me < n_seq - 1)
-
-    @pl.when(sends_near)
-    def _():
-        near_copy().start()
+    feeds_short = (me >= n_long) & (me < n_real - 1)
+
+    @pl.when(is_late)
+    def _():
+        @pl.loop(me + 1, n_long)
+        def _(d):
+            near_copy(d, me - n_early, d - me - 1).start()
+
+    @pl.when(feeds_short)
+    def _():
+        near_copy(me + 1, 0, 0).start()
 
     for pair in range(heads // 2):
         both = jnp.concatenate([qkv[2 * pair, HD:, :], qkv[2 * pair + 1, HD:, :]], axis=0)
@@ -231,15 +254,15 @@
 
     def first(scores, values):
         top = jnp.max(scores, axis=0, keepdims=True)
-        weights = jnp.exp2((scores - top) * SCALE2)
+        weights = jnp.exp((scores - top) * SCALE)
         total = jnp.sum(weights, axis=0, keepdims=True)
         return top, total, jnp.dot(values, weights.astype(BF16), preferred_element_type=F32)
 
     def more(state, scores, values):
         top, total, context = state
         new_top = jnp.maximum(top, jnp.max(scores, axis=0, keepdims=True))
-        factor = jnp.exp2((top - new_top) * SCALE2)
-        weights = jnp.exp2((scores - new_top) * SCALE2)
+        factor = jnp.exp((top - new_top) * SCALE)
+        weights = jnp.exp((scores - new_top) * SCALE)
         total = factor * total + jnp.sum(weights, axis=0, keepdims=True)
         context = factor * context + jnp.dot(
             values, weights.astype(BF16), preferred_element_type=F32
@@ -264,7 +287,23 @@
 
     @pl.when(me < heads)
     def _():
-        @pl.loop(0, n_long)
+        def several(query, count, start):
+            def step(i, state):
+                blocks = [start + i * count + b for b in range(count)]
+                scores = jnp.concatenate(
+                    [jnp.dot(krow[b], query, preferred_element_type=F32) for b in blocks], axis=0
+                )
+                values = jnp.concatenate([inbuf[b, 2 * HD:, :] for b in blocks], axis=1)
+                return first(scores, values) if state is None else more(state, scores, values)
+
+            return step
+
+        def finish(j, state):
+            top, total, context = state
+            obuf[j] = (context / total).astype(BF16)
+            lbuf[j] = jnp.broadcast_to(top * SCALE + jnp.log(total), lbuf.shape[1:])
+
+        @pl.loop(0, n_early)
         def _(j):
             @pl.when(j != me)
             def _():
@@ -276,31 +315,13 @@
 
             krow[j] = inbuf[j, HD:2 * HD, :].T
             query = inbuf[j, :HD, :]
-
-            def score(i):
-                return jnp.dot(krow[i], query, preferred_element_type=F32)
-
-            def value(i):
-                return inbuf[i, 2 * HD:, :]
-
-            state = first(jnp.where(key_iota <= query_iota, score(j), LOW), value(j))
-
-            def several(count, start):
-                def step(i, state):
-                    blocks = [start + i * count + b for b in range(count)]
-                    scores = jnp.concatenate([score(b) for b in blocks], axis=0)
-                    values = jnp.concatenate([value(b) for b in blocks], axis=1)
-                    return more(state, scores, values)
-
-                return step
-
-            state = lax.fori_loop(0, j // 4, several(4, 0), state)
+            scores = jnp.dot(krow[j], query, preferred_element_type=F32)
+            state = first(jnp.where(key_iota <= query_iota, scores, LOW), inbuf[j, 2 * HD:, :])
+            state = lax.fori_loop(0, j // 4, several(query, 4, 0), state)
             left = lax.rem(j, 4)
-            state = lax.fori_loop(0, left // 2, several(2, j - left), state)
-            state = lax.fori_loop(0, lax.rem(j, 2), several(1, j - 1), state)
-            top, total, context = state
-            obuf[j] = (context / total).astype(BF16)
-            lbuf[j] = jnp.broadcast_to(top * (SCALE2 * LN2) + jnp.log(total), lbuf.shape[1:])
+            state = lax.fori_loop(0, left // 2, several(query, 2, j - left), state)
+            state = lax.fori_loop(0, lax.rem(j, 2), several(query, 1, j - 1), state)
+            finish(j, state)
 
             @pl.when(j != me)
             def _():
@@ -312,24 +333,69 @@
                 pltpu.make_async_copy(obuf.at[me], att_ref.at[me], arecv.at[me]).start()
                 pltpu.make_async_copy(lbuf.at[me], lse_ref.at[me], mrecv.at[me]).start()
 
-    @pl.when(me >= n_long)
-    def _():
-        near_copy().wait_recv()
+        @pl.loop(n_early, n_long)
+        def _(j):
+            query_copy(0, j).wait_recv()
+            query = late[j - n_early]
+            state = several(query, 4, 0)(0, None)
+            finish(j, lax.fori_loop(1, n_early // 4, several(query, 4, 0), state))
+            for copy in answer_copies(j, me):
+                copy.start()
+
+    @pl.when(is_late | is_short)
+    def _():
+        slots = jnp.where(is_late, me - n_early, jnp.where(me > n_long, 1, 0))
+
+        @pl.loop(0, slots)
+        def _(slot):
+            near_copy(0, slot, 0).wait_recv()
 
         @pl.loop(0, heads)
         def _(h):
             query = qkv[h, :HD, :]
             here = jnp.dot(qkv[h, HD:2 * HD, :].T, query, preferred_element_type=F32)
-            there = jnp.dot(near[h, :HD, :].T, query, preferred_element_type=F32)
             here = jnp.where((key_iota <= query_iota) & (key_iota >= begin), here, LOW)
-            there = jnp.where(key_iota - tok >= begin, there, LOW)
-            values = jnp.concatenate([near[h, HD:, :], qkv[h, 2 * HD:, :]], axis=1)
-            top, total, context = first(jnp.concatenate([there, here], axis=0), values)
-            att_ref[h] = jnp.where(padding, 0.0, context / total).astype(BF16)
-            logs = jnp.where(padding, 0.0, top * (SCALE2 * LN2) + jnp.log(total))
-            lse_ref[h] = jnp.broadcast_to(logs, lse_ref.shape[1:])
-
-    @pl.when(me < n_long)
+
+            def before(slot, state):
+                there = jnp.dot(near[slot, h, :HD, :].T, query, preferred_element_type=F32)
+                there = jnp.where(key_iota - (slots - slot) * tok >= begin, there, LOW)
+                return more(state, there, near[slot, h, HD:, :])
+
+            state = lax.fori_loop(0, slots, before, first(here, qkv[h, 2 * HD:, :]))
+            top, total, context = state
+            context = context / total
+            logs = top * SCALE + jnp.log(total)
+            local[h] = context
+            logged[h] = jnp.broadcast_to(logs, logged.shape[1:])
+
+        @pl.when(is_short)
+        def _():
+            @pl.loop(0, heads)
+            def _(h):
+                att_ref[h] = jnp.where(padding, 0.0, local[h]).astype(BF16)
+                lse_ref[h] = jnp.where(padding, 0.0, logged[h])
+
+        @pl.when(is_late)
+        def _():
+            @pl.loop(0, heads)
+            def _(h):
+                for copy in answer_copies(0, h):
+                    copy.wait_recv()
+                logs_here = logged[h, 0:1, :]
+                logs_there = lse_ref[h, 0:1, :]
+                most = jnp.maximum(logs_here, logs_there)
+                logs = most + jnp.log(jnp.exp(logs_here - most) + jnp.exp(logs_there - most))
+                merged = local[h] * jnp.exp(logs_here - logs)
+                merged = merged + att_ref[h].astype(F32) * jnp.exp(logs_there - logs)
+                att_ref[h] = merged.astype(BF16)
+                lse_ref[h] = jnp.broadcast_to(logs, lse_ref.shape[1:])
+
+    @pl.when(me >= n_real)
+    def _():
+        att_ref[...] = jnp.zeros_like(att_ref)
+        lse_ref[...] = jnp.zeros_like(lse_ref)
+
+    @pl.when(me < n_early)
     def _():
         @pl.loop(0, heads)
         def _(h):
@@ -346,7 +412,7 @@
     for r in range(1, n_head):
         feature_copy(r).wait_send()
 
-    @pl.when(me < n_long)
+    @pl.when(me < n_early)
     def _():
         @pl.loop(0, heads)
         def _(h):
@@ -354,9 +420,19 @@
             def _():
                 long_copy(h, me).wait_send()
 
-    @pl.when(sends_near)
-    def _():
-        near_copy().wait_send()
+    @pl.when(is_late)
+    def _():
+        @pl.loop(0, heads)
+        def _(h):
+            query_copy(h, me).wait_send()
+
+        @pl.loop(me + 1, n_long)
+        def _(d):
+            near_copy(d, me - n_early, d - me - 1).wait_send()
+
+    @pl.when(feeds_short)
+    def _():
+        near_copy(me + 1, 0, 0).wait_send()
 
     @pl.when(me < heads)
     def _():
@@ -393,6 +469,8 @@
     n_long = n_seq * 11 // 16
     cap = 2 * tok // n_seq
     pages = tok // cap
+    n_early = n_seq // 2
+    slots = max(n_long - n_early - 1, 1)
     width = 256 if cols % 256 == 0 else cols
     tiles = cols // width
 
@@ -419,19 +497,22 @@
             pltpu.VMEM((heads, PART, tok), BF16),
             pltpu.VMEM((pages + 1, cap, heads * 2 * HD), BF16),
             pltpu.VMEM((n_seq, cap, heads * 2 * HD), BF16),
-            pltpu.VMEM((n_long, PART, tok), BF16),
-            pltpu.VMEM((n_long, tok, HD), BF16),
-            pltpu.VMEM((heads, 2 * HD, tok), BF16),
+            pltpu.VMEM((n_early, PART, tok), BF16),
+            pltpu.VMEM((n_long - n_early, HD, tok), BF16),
+            pltpu.VMEM((n_early, tok, HD), BF16),
+            pltpu.VMEM((slots, heads, 2 * HD, tok), BF16),
             pltpu.VMEM((n_long, HD, tok), BF16),
             pltpu.VMEM((n_long, 8, tok), F32),
+            pltpu.VMEM((heads, HD, tok), F32),
+            pltpu.VMEM((heads, 8, tok), F32),
             dma((tiles,)),
             dma,
             dma((n_head - 1,)),
             dma((n_head - 1,)),
             dma((heads,)),
             dma((n_long,)),
-            dma,
-            dma,
+            dma((slots,)),
+            dma((slots,)),
             dma((n_seq,)),
             dma((n_seq,)),
             dma((n_long,)),
@@ -440,7 +521,7 @@
             dma((heads,)),
         ],
         compiler_params=pltpu.CompilerParams(
-            collective_id=0, has_side_effects=True, vmem_limit_bytes=60 * 1024 * 1024
+            collective_id=0, has_side_effects=True, vmem_limit_bytes=50 * 1024 * 1024
         ),
         cost_estimate=pl.CostEstimate(
             flops=2 * tok * feat * n_head * cols, bytes_accessed=2 * feat * n_head * cols,

time: 83.9 us -> 84.1 us (level)
  the two profiles are of different devices: /device:TPU:15 before, /device:TPU:20 now
where the time goes in v4:
time: 84.1 us; the launch traced here: 83.5 us
  Pallas kernels  77 us (92%)
  local copies, waits for them, and re-layouts  5.87 us (7%)
    pallas_call x1, Pallas kernels, body(): pl.pallas_call(functools.partial(kernel, n_seq, n_head, n_long), out_shap...  77 us
    unnamed x10, local copies, waits for them, and re-layouts  4.94 us

profile of v4, /device:TPU:20, one launch (start us, length us, event | category | flops | bytes accessed | tf_op | source)
XLA Modules:
  0.0 83.5 jit_solution(10176262235995553661)
XLA Ops:
  0.6 0.0 copy-start
  0.6 1.1 %copy-done = bf16[256,1536]{1,0:T(8,128)(2,1)S(1)} copy-done((bf16[256,1536]{1,0:T(8,128)(2,1)S(1)}, bf16[256,1536]{1,0:T(8,128)(2,1)}, u32[]{:S(2)}) %copy-start) | copy-done | bytes 786456
  1.8 0.0 copy-start.1
  1.8 0.7 copy-done.1
  2.5 0.0 copy-start.2
  2.5 0.7 copy-done.2
  3.2 0.0 copy-start.3
  3.2 0.7 copy-done.3
  3.8 77.0 %shard_map.76 = (bf16[8,96,256]{2,1,0:T(8,128)(2,1)S(1)}, f32[8,8,256]{2,1,0:T(8,128)S(1)}, bf16[16,32,1536]{2,1,0:T(8,128)(2,1)S(1)}) custom-call(s32[8]{0:T(128)S(1)} %copy-done.3, s32[256]{0:T(256)S(1)} %bitcast.9, f32[48,1]{1,0:T(8,128)S(1)} %copy-done.1, bf16[256,1536]{1,0:T(8,128)(2,1)S(1)} %copy-done, bf16[3072,2304]{1,0:T(8,128)(2,1)} %w_ref.1), custom_call_target="tpu_custom_call" | custom-call | flops 3623878656 | bytes 14155776 | tf_op jit(solution)/shard_map/pallas_call | solution.py:482
  80.9 0.9 %copy.8 = bf16[768,256]{0,1:T(8,128)(2,1)} copy(bf16[768,256]{1,0:T(8,128)(2,1)S(1)} %bitcast.8) | data formatting | bytes 786432 | tf_op jit(solution)/shard_map/reshape | solution.py:533
  81.8 0.6 copy.11
  82.4 1.1 %copy.13 = bf16[512,1536]{1,0:T(8,128)(2,1)} copy(bf16[512,1536]{1,0:T(8,128)(2,1)S(1)} %bitcast.7) | data formatting | bytes 3145728
  (1 shorter events, 0.0 us)
Async XLA Ops:
  0.6 1.1 %copy-start = (bf16[256,1536]{1,0:T(8,128)(2,1)S(1)}, bf16[256,1536]{1,0:T(8,128)(2,1)}, u32[]{:S(2)}) copy-start(bf16[256,1536]{1,0:T(8,128)(2,1)} %x_ref.1) | copy-start | bytes 2359300
  1.8 0.7 copy-start.1
  2.5 0.7 copy-start.2
  3.2 0.7 copy-start.3

commit v5 on v4

--- a/solution.py
+++ b/solution.py
@@ -43,7 +43,7 @@
 
 def kernel(
     n_seq, n_head, n_long,
-    short_ref, owner_ref, freq_ref, x_ref, w_ref,
+    short_ref, owner_ref, x_ref, w_ref,
     att_ref, lse_ref, kv_ref,
     wbuf, xbuf, proj, cosine, sine, qkv, rows, outbox, inbuf, late, krow, near, obuf, lbuf, local, logged,
     wsem, xown, xsend, xrecv, lsend, lrecv, nsend, nrecv, csend, crecv, asend, arecv, msend, mrecv,
@@ -57,6 +57,8 @@
     pages = rows.shape[0] - 1
     n_real = n_long + n_seq // 4
     n_early = inbuf.shape[0]
+    last_slot = n_long - n_early - 2
+    half = n_seq // 2
 
     def weight_copy(c):
         return pltpu.make_async_copy(
@@ -90,7 +92,11 @@
         padding = row_ids >= bound
         if j < short_ref.shape[0]:
             bound = bound + short_ref[j]
-    angle = freq_ref[...] * (row_ids - begin).astype(F32)
+    line = lax.broadcasted_iota(jnp.int32, (HALF, tok), 0)
+    inverse_freq = jnp.ones((HALF, tok), F32)
+    for i in range(1, HALF):
+        inverse_freq = jnp.where(line == i, float(np.float32(rope_base ** (-i / HALF))), inverse_freq)
+    angle = inverse_freq * (row_ids - begin).astype(F32)
     begin = begin - first_row
     cos_value, sin_value = circular(angle)
     cosine[...] = cos_value
@@ -193,13 +199,31 @@
             device_id_type=MESH,
         )
 
+    def relay_copy():
+        return pltpu.make_async_remote_copy(
+            src_ref=near.at[0],
+            dst_ref=near.at[last_slot],
+            send_sem=nsend.at[last_slot],
+            recv_sem=nrecv.at[last_slot],
+            device_id={"seq": n_long - 1},
+            device_id_type=MESH,
+        )
+
     feeds_short = (me >= n_long) & (me < n_real - 1)
 
     @pl.when(is_late)
     def _():
         @pl.loop(me + 1, n_long)
         def _(d):
-            near_copy(d, me - n_early, d - me - 1).start()
+            relayed = (me == n_long - 2) & (d == n_long - 1)
+
+            @pl.when(relayed)
+            def _():
+                near_copy(n_long, 0, 0).start()
+
+            @pl.when(jnp.logical_not(relayed))
+            def _():
+                near_copy(d, me - n_early, d - me - 1).start()
 
     @pl.when(feeds_short)
     def _():
@@ -245,9 +269,15 @@
 
     @pl.when(me < n_real)
     def _():
-        @pl.loop(1, n_seq)
+        own_half = half * (me // half)
+
+        @pl.loop(0, half)
         def _(k):
-            cache_copy(lax.rem(me + k, n_seq), me).start()
+            cache_copy(half - own_half + lax.rem(me + k, half), me).start()
+
+        @pl.loop(1, half)
+        def _(k):
+            cache_copy(own_half + lax.rem(me + k, half), me).start()
 
     query_iota = lax.broadcasted_iota(jnp.int32, (tok, tok), 1)
     key_iota = lax.broadcasted_iota(jnp.int32, (tok, tok), 0)
@@ -301,7 +331,7 @@
         def finish(j, state):
             top, total, context = state
             obuf[j] = (context / total).astype(BF16)
-            lbuf[j] = jnp.broadcast_to(top * SCALE + jnp.log(total), lbuf.shape[1:])
+            lbuf[j] = top * SCALE + jnp.log(total)
 
         @pl.loop(0, n_early)
         def _(j):
@@ -342,6 +372,11 @@
             for copy in answer_copies(j, me):
                 copy.start()
 
+    @pl.when(me == n_long)
+    def _():
+        near_copy(0, 0, 0).wait_recv()
+        relay_copy().start()
+
     @pl.when(is_late | is_short)
     def _():
         slots = jnp.where(is_late, me - n_early, jnp.where(me > n_long, 1, 0))
@@ -366,7 +401,7 @@
             context = context / total
             logs = top * SCALE + jnp.log(total)
             local[h] = context
-            logged[h] = jnp.broadcast_to(logs, logged.shape[1:])
+            logged[h] = logs
 
         @pl.when(is_short)
         def _():
@@ -381,14 +416,14 @@
             def _(h):
                 for copy in answer_copies(0, h):
                     copy.wait_recv()
-                logs_here = logged[h, 0:1, :]
-                logs_there = lse_ref[h, 0:1, :]
+                logs_here = logged[h]
+                logs_there = lse_ref[h]
                 most = jnp.maximum(logs_here, logs_there)
                 logs = most + jnp.log(jnp.exp(logs_here - most) + jnp.exp(logs_there - most))
                 merged = local[h] * jnp.exp(logs_here - logs)
                 merged = merged + att_ref[h].astype(F32) * jnp.exp(logs_there - logs)
                 att_ref[h] = merged.astype(BF16)
-                lse_ref[h] = jnp.broadcast_to(logs, lse_ref.shape[1:])
+                lse_ref[h] = logs
 
     @pl.when(me >= n_real)
     def _():
@@ -433,6 +468,10 @@
     @pl.when(feeds_short)
     def _():
         near_copy(me + 1, 0, 0).wait_send()
+
+    @pl.when(me == n_long)
+    def _():
+        relay_copy().wait_send()
 
     @pl.when(me < heads)
     def _():
@@ -470,11 +509,10 @@
     cap = 2 * tok // n_seq
     pages = tok // cap
     n_early = n_seq // 2
-    slots = max(n_long - n_early - 1, 1)
+    slots = n_long - n_early - 1
     width = 256 if cols % 256 == 0 else cols
     tiles = cols // width
 
-    inverse_freq = (rope_base ** (-np.arange(HALF) / HALF)).astype(np.float32)[:, None]
     smem = pl.BlockSpec(memory_space=pltpu.SMEM)
     vmem = pl.BlockSpec(memory_space=pltpu.VMEM)
     hbm = pl.BlockSpec(memory_space=pl.ANY)
@@ -483,10 +521,10 @@
         functools.partial(kernel, n_seq, n_head, n_long),
         out_shape=(
             jax.ShapeDtypeStruct((heads, HD, tok), BF16),
-            jax.ShapeDtypeStruct((heads, 8, tok), F32),
+            jax.ShapeDtypeStruct((heads, 1, tok), F32),
             jax.ShapeDtypeStruct((n_seq, cap, heads * 2 * HD), BF16),
         ),
-        in_specs=[smem, smem, vmem, hbm, hbm],
+        in_specs=[smem, smem, hbm, hbm],
         out_specs=(vmem, vmem, hbm),
         scratch_shapes=[
             pltpu.VMEM((tiles, n_head * feat, width), BF16),
@@ -502,9 +540,9 @@
             pltpu.VMEM((n_early, tok, HD), BF16),
             pltpu.VMEM((slots, heads, 2 * HD, tok), BF16),
             pltpu.VMEM((n_long, HD, tok), BF16),
-            pltpu.VMEM((n_long, 8, tok), F32),
+            pltpu.VMEM((n_long, 1, tok), F32),
             pltpu.VMEM((heads, HD, tok), F32),
-            pltpu.VMEM((heads, 8, tok), F32),
+            pltpu.VMEM((heads, 1, tok), F32),
             dma((tiles,)),
             dma,
             dma((n_head - 1,)),
@@ -528,10 +566,10 @@
             transcendentals=0,
         ),
     )(
-        short_lengths, cache_owner.reshape(tok), jnp.asarray(inverse_freq), stream_x, qkv_weight,
+        short_lengths, cache_owner.reshape(tok), stream_x, qkv_weight,
     )
     attended = attended.reshape(heads * HD, tok).T
-    return attended, row_lse[:, 0, :], cache.reshape(n_seq * cap, heads * 2 * HD)
+    return attended, row_lse.reshape(heads, tok), cache.reshape(n_seq * cap, heads * 2 * HD)
 
 
 def solution(mesh):

time: 84.1 us -> 78.9 us (0.938)
  Pallas kernels: 77 us -> 72.6 us
    pallas_call x1, Pallas kernels: 77 us -> 72.6 us  [body(): pl.pallas_call(functools.partial(kernel, n_seq, n_head, n_long), out_shap...]
    unnamed x10 -> x8, local copies, waits for them, and re-layouts: 4.94 us -> 4.2 us
where the time goes in v5:
time: 78.9 us; the launch traced here: 78.4 us
  Pallas kernels  72.6 us (92%)
  local copies, waits for them, and re-layouts  5.12 us (6%)
    pallas_call x1, Pallas kernels, body(): pl.pallas_call(functools.partial(kernel, n_seq, n_head, n_long), out_shap...  72.6 us
    unnamed x8, local copies, waits for them, and re-layouts  4.2 us

profile of v5, /device:TPU:20, one launch (start us, length us, event | category | flops | bytes accessed | tf_op | source)
XLA Modules:
  0.0 78.4 jit_solution(8754951275678563065)
XLA Ops:
  0.6 0.0 copy-start
  0.6 1.1 %copy-done = bf16[256,1536]{1,0:T(8,128)(2,1)S(1)} copy-done((bf16[256,1536]{1,0:T(8,128)(2,1)S(1)}, bf16[256,1536]{1,0:T(8,128)(2,1)}, u32[]{:S(2)}) %copy-start) | copy-done | bytes 786456
  1.8 0.0 copy-start.1
  1.8 0.7 copy-done.1
  2.4 0.0 copy-start.2
  2.4 0.7 copy-done.2
  3.1 72.6 %shard_map.67 = (bf16[8,96,256]{2,1,0:T(8,128)(2,1)S(1)}, f32[8,1,256]{2,1,0:T(1,128)S(1)}, bf16[16,32,1536]{2,1,0:T(8,128)(2,1)S(1)}) custom-call(s32[8]{0:T(128)S(1)} %copy-done.2, s32[256]{0:T(256)S(1)} %bitcast.9, bf16[256,1536]{1,0:T(8,128)(2,1)S(1)} %copy-done, bf16[3072,2304]{1,0:T(8,128)(2,1)} %w_ref.1), custom_call_target="tpu_custom_call" | custom-call | flops 3623878656 | bytes 14155776 | tf_op jit(solution)/shard_map/pallas_call | solution.py:520
  75.7 0.9 %copy.7 = bf16[768,256]{0,1:T(8,128)(2,1)} copy(bf16[768,256]{1,0:T(8,128)(2,1)S(1)} %bitcast.8) | data formatting | bytes 786432 | tf_op jit(solution)/shard_map/reshape | solution.py:571
  76.7 0.6 copy.10
  77.3 1.1 %copy.12 = bf16[512,1536]{1,0:T(8,128)(2,1)} copy(bf16[512,1536]{1,0:T(8,128)(2,1)S(1)} %bitcast.7) | data formatting | bytes 3145728
Async XLA Ops:
  0.6 1.1 %copy-start = (bf16[256,1536]{1,0:T(8,128)(2,1)S(1)}, bf16[256,1536]{1,0:T(8,128)(2,1)}, u32[]{:S(2)}) copy-start(bf16[256,1536]{1,0:T(8,128)(2,1)} %x_ref.1) | copy-start | bytes 2359300
  1.8 0.7 copy-start.1
  2.4 0.7 copy-start.2

commit v6 on v5

--- a/solution.py
+++ b/solution.py
@@ -45,7 +45,7 @@
     n_seq, n_head, n_long,
     short_ref, owner_ref, x_ref, w_ref,
     att_ref, lse_ref, kv_ref,
-    wbuf, xbuf, proj, cosine, sine, qkv, rows, outbox, inbuf, late, krow, near, obuf, lbuf, local, logged,
+    wbuf, xbuf, proj, cosine, sine, qkv, rows, outbox, inbuf, late, krow, near, obuf, lbuf, local, logged, tops,
     wsem, xown, xsend, xrecv, lsend, lrecv, nsend, nrecv, csend, crecv, asend, arecv, msend, mrecv,
 ):
     me = lax.axis_index("seq")
@@ -53,8 +53,9 @@
     tok, feat = x_ref.shape
     heads = qkv.shape[0]
     tiles, _, width = wbuf.shape
-    cap = outbox.shape[1]
-    pages = rows.shape[0] - 1
+    groups, _, cap, group_width = outbox.shape
+    pages = rows.shape[1] - 1
+    group_heads = heads // groups
     n_real = n_long + n_seq // 4
     n_early = inbuf.shape[0]
     last_slot = n_long - n_early - 2
@@ -154,8 +155,7 @@
     is_late = (me >= n_early) & (me < n_long)
     is_short = (me >= n_long) & (me < n_real)
 
-    @pl.loop(0, tiles)
-    def _(c):
+    def project(c):
         weight_copy(c).wait()
         part = jnp.zeros((tok, width), F32)
         for r in range(n_head):
@@ -189,6 +189,71 @@
             def _():
                 pltpu.make_async_copy(qkv.at[me], inbuf.at[me], lrecv.at[me]).start()
 
+    def cache_copy(g, owner, source):
+        return pltpu.make_async_remote_copy(
+            src_ref=outbox.at[g, owner],
+            dst_ref=kv_ref.at[source, :, pl.ds(g * group_width, group_width)],
+            send_sem=csend.at[g, owner],
+            recv_sem=crecv.at[g, source],
+            device_id={"seq": owner},
+            device_id_type=MESH,
+        )
+
+    def own_slot(g):
+        return pltpu.make_async_copy(
+            outbox.at[g, me],
+            kv_ref.at[me, :, pl.ds(g * group_width, group_width)],
+            crecv.at[g, me],
+        )
+
+    def zero_slot(g, s):
+        return pltpu.make_async_copy(
+            rows.at[g, pages],
+            kv_ref.at[s, :, pl.ds(g * group_width, group_width)],
+            crecv.at[g, s],
+        )
+
+    own_half = half * (me // half)
+
+    def send_slots(g):
+        for pair in range(group_heads // 2):
+            h = g * group_heads + 2 * pair
+            turned = jnp.concatenate([qkv[h, HD:, :], qkv[h + 1, HD:, :]], axis=0).T
+            for p in range(pages):
+                rows[g, p, :, pair * 4 * HD:(pair + 1) * 4 * HD] = turned[p * cap:(p + 1) * cap, :]
+        rows[g, pages] = jnp.zeros(rows.shape[2:], BF16)
+
+        @pl.loop(0, n_seq)
+        def _(o):
+            page = pages
+            for p in range(pages):
+                page = jnp.where(owner_ref[p * cap] == o, p, page)
+            outbox[g, o] = rows[g, page]
+
+        @pl.when(me < n_real)
+        def _():
+            own_slot(g).start()
+
+            @pl.loop(0, half)
+            def _(k):
+                cache_copy(g, half - own_half + lax.rem(me + k, half), me).start()
+
+            @pl.loop(1, half)
+            def _(k):
+                cache_copy(g, own_half + lax.rem(me + k, half), me).start()
+
+        @pl.loop(n_real, n_seq)
+        def _(s):
+            zero_slot(g, s).start()
+
+    first_tile = 0
+    for g in range(groups):
+        last_tile = min(tiles, -(-(g + 1) * group_heads * PART // width))
+        pl.loop(first_tile, last_tile)(project)
+        first_tile = last_tile
+        if g < groups - 1:
+            send_slots(g)
+
     def near_copy(target, slot, send_slot):
         return pltpu.make_async_remote_copy(
             src_ref=qkv.at[:, pl.ds(HD, 2 * HD)],
@@ -229,55 +294,7 @@
     def _():
         near_copy(me + 1, 0, 0).start()
 
-    for pair in range(heads // 2):
-        both = jnp.concatenate([qkv[2 * pair, HD:, :], qkv[2 * pair + 1, HD:, :]], axis=0)
-        turned = both.T
-        for p in range(pages):
-            rows[p, :, pair * 4 * HD:(pair + 1) * 4 * HD] = turned[p * cap:(p + 1) * cap, :]
-    rows[pages] = jnp.zeros(rows.shape[1:], BF16)
-
-    def cache_copy(owner, source):
-        return pltpu.make_async_remote_copy(
-            src_ref=outbox.at[owner],
-            dst_ref=kv_ref.at[source],
-            send_sem=csend.at[owner],
-            recv_sem=crecv.at[source],
-            device_id={"seq": owner},
-            device_id_type=MESH,
-        )
-
-    @pl.loop(0, n_seq)
-    def _(o):
-        page = pages
-        for p in range(pages):
-            page = jnp.where(owner_ref[p * cap] == o, p, page)
-        outbox[o] = rows[page]
-
-    def own_slot():
-        return pltpu.make_async_copy(outbox.at[me], kv_ref.at[me], crecv.at[me])
-
-    def zero_slot(s):
-        return pltpu.make_async_copy(rows.at[pages], kv_ref.at[s], crecv.at[s])
-
-    @pl.when(me < n_real)
-    def _():
-        own_slot().start()
-
-    @pl.loop(n_real, n_seq)
-    def _(s):
-        zero_slot(s).start()
-
-    @pl.when(me < n_real)
-    def _():
-        own_half = half * (me // half)
-
-        @pl.loop(0, half)
-        def _(k):
-            cache_copy(half - own_half + lax.rem(me + k, half), me).start()
-
-        @pl.loop(1, half)
-        def _(k):
-            cache_copy(own_half + lax.rem(me + k, half), me).start()
+    send_slots(groups - 1)
 
     query_iota = lax.broadcasted_iota(jnp.int32, (tok, tok), 1)
     key_iota = lax.broadcasted_iota(jnp.int32, (tok, tok), 0)
@@ -381,27 +398,31 @@
     def _():
         slots = jnp.where(is_late, me - n_early, jnp.where(me > n_long, 1, 0))
 
+        def keep(h, state):
+            tops[h], logged[h], local[h] = state
+
+        @pl.loop(0, heads)
+        def _(h):
+            here = jnp.dot(qkv[h, HD:2 * HD, :].T, qkv[h, :HD, :], preferred_element_type=F32)
+            here = jnp.where((key_iota <= query_iota) & (key_iota >= begin), here, LOW)
+            keep(h, first(here, qkv[h, 2 * HD:, :]))
+
         @pl.loop(0, slots)
         def _(slot):
             near_copy(0, slot, 0).wait_recv()
 
+            @pl.loop(0, heads)
+            def _(h):
+                there = jnp.dot(
+                    near[slot, h, :HD, :].T, qkv[h, :HD, :], preferred_element_type=F32
+                )
+                there = jnp.where(key_iota - (slots - slot) * tok >= begin, there, LOW)
+                keep(h, more((tops[h], logged[h], local[h]), there, near[slot, h, HD:, :]))
+
         @pl.loop(0, heads)
         def _(h):
-            query = qkv[h, :HD, :]
-            here = jnp.dot(qkv[h, HD:2 * HD, :].T, query, preferred_element_type=F32)
-            here = jnp.where((key_iota <= query_iota) & (key_iota >= begin), here, LOW)
-
-            def before(slot, state):
-                there = jnp.dot(near[slot, h, :HD, :].T, query, preferred_element_type=F32)
-                there = jnp.where(key_iota - (slots - slot) * tok >= begin, there, LOW)
-                return more(state, there, near[slot, h, HD:, :])
-
-            state = lax.fori_loop(0, slots, before, first(here, qkv[h, 2 * HD:, :]))
-            top, total, context = state
-            context = context / total
-            logs = top * SCALE + jnp.log(total)
-            local[h] = context
-            logged[h] = logs
+            local[h] = local[h] / logged[h]
+            logged[h] = tops[h] * SCALE + jnp.log(logged[h])
 
         @pl.when(is_short)
         def _():
@@ -482,23 +503,24 @@
                 for copy in answer_copies(j, me):
                     copy.wait_send()
 
-    @pl.when(me < n_real)
-    def _():
-        own_slot().wait()
-
-        @pl.loop(1, n_seq)
-        def _(k):
-            cache_copy(lax.rem(me + k, n_seq), me).wait_send()
-
-    @pl.loop(0, n_real)
-    def _(s):
-        @pl.when(s != me)
-        def _():
-            cache_copy(s, s).wait_recv()
-
-    @pl.loop(n_real, n_seq)
-    def _(s):
-        zero_slot(s).wait()
+    for g in range(groups):
+        @pl.when(me < n_real)
+        def _(g=g):
+            own_slot(g).wait()
+
+            @pl.loop(1, n_seq)
+            def _(k):
+                cache_copy(g, lax.rem(me + k, n_seq), me).wait_send()
+
+        @pl.loop(0, n_real)
+        def _(s, g=g):
+            @pl.when(s != me)
+            def _():
+                cache_copy(g, s, s).wait_recv()
+
+        @pl.loop(n_real, n_seq)
+        def _(s, g=g):
+            zero_slot(g, s).wait()
 
 
 def body(n_seq, n_head, stream_x, qkv_weight, short_lengths, cache_owner):
@@ -509,6 +531,8 @@
     cap = 2 * tok // n_seq
     pages = tok // cap
     n_early = n_seq // 2
+    groups = 2 if heads % 4 == 0 else 1
+    group_width = heads // groups * 2 * HD
     slots = n_long - n_early - 1
     width = 256 if cols % 256 == 0 else cols
     tiles = cols // width
@@ -533,8 +557,8 @@
             pltpu.VMEM((HALF, tok), F32),
             pltpu.VMEM((HALF, tok), F32),
             pltpu.VMEM((heads, PART, tok), BF16),
-            pltpu.VMEM((pages + 1, cap, heads * 2 * HD), BF16),
-            pltpu.VMEM((n_seq, cap, heads * 2 * HD), BF16),
+            pltpu.VMEM((groups, pages + 1, cap, group_width), BF16),
+            pltpu.VMEM((groups, n_seq, cap, group_width), BF16),
             pltpu.VMEM((n_early, PART, tok), BF16),
             pltpu.VMEM((n_long - n_early, HD, tok), BF16),
             pltpu.VMEM((n_early, tok, HD), BF16),
@@ -542,6 +566,7 @@
             pltpu.VMEM((n_long, HD, tok), BF16),
             pltpu.VMEM((n_long, 1, tok), F32),
             pltpu.VMEM((heads, HD, tok), F32),
+            pltpu.VMEM((heads, 1, tok), F32),
             pltpu.VMEM((heads, 1, tok), F32),
             dma((tiles,)),
             dma,
@@ -551,8 +576,8 @@
             dma((n_long,)),
             dma((slots,)),
             dma((slots,)),
-            dma((n_seq,)),
-            dma((n_seq,)),
+            dma((groups, n_seq)),
+            dma((groups, n_seq)),
             dma((n_long,)),
             dma((heads,)),
             dma((n_long,)),

time: 78.9 us -> 78.6 us (level)
  no operation moved by 1% of the time
where the time goes in v6:
time: 78.6 us; the launch traced here: 78.4 us
  Pallas kernels  72.6 us (92%)
  local copies, waits for them, and re-layouts  5.12 us (7%)
    pallas_call x1, Pallas kernels, body(): pl.pallas_call(functools.partial(kernel, n_seq, n_head, n_long), out_shap...  72.6 us
    unnamed x8, local copies, waits for them, and re-layouts  4.2 us

profile of v6, /device:TPU:20, one launch (start us, length us, event | category | flops | bytes accessed | tf_op | source)
XLA Modules:
  0.0 78.4 jit_solution(3342989219955496893)
XLA Ops:
  0.6 0.0 copy-start
  0.6 1.1 %copy-done = bf16[256,1536]{1,0:T(8,128)(2,1)S(1)} copy-done((bf16[256,1536]{1,0:T(8,128)(2,1)S(1)}, bf16[256,1536]{1,0:T(8,128)(2,1)}, u32[]{:S(2)}) %copy-start) | copy-done | bytes 786456
  1.8 0.0 copy-start.1
  1.8 0.7 copy-done.1
  2.4 0.0 copy-start.2
  2.4 0.7 copy-done.2
  3.1 72.6 %shard_map.67 = (bf16[8,96,256]{2,1,0:T(8,128)(2,1)S(1)}, f32[8,1,256]{2,1,0:T(1,128)S(1)}, bf16[16,32,1536]{2,1,0:T(8,128)(2,1)S(1)}) custom-call(s32[8]{0:T(128)S(1)} %copy-done.2, s32[256]{0:T(256)S(1)} %bitcast.9, bf16[256,1536]{1,0:T(8,128)(2,1)S(1)} %copy-done, bf16[3072,2304]{1,0:T(8,128)(2,1)} %w_ref.1), custom_call_target="tpu_custom_call" | custom-call | flops 3623878656 | bytes 14155776 | tf_op jit(solution)/shard_map/pallas_call | solution.py:544
  75.7 0.9 %copy.7 = bf16[768,256]{0,1:T(8,128)(2,1)} copy(bf16[768,256]{1,0:T(8,128)(2,1)S(1)} %bitcast.8) | data formatting | bytes 786432 | tf_op jit(solution)/shard_map/reshape | solution.py:596
  76.7 0.6 copy.10
  77.3 1.1 %copy.12 = bf16[512,1536]{1,0:T(8,128)(2,1)} copy(bf16[512,1536]{1,0:T(8,128)(2,1)S(1)} %bitcast.7) | data formatting | bytes 3145728
Async XLA Ops:
  0.6 1.1 %copy-start = (bf16[256,1536]{1,0:T(8,128)(2,1)S(1)}, bf16[256,1536]{1,0:T(8,128)(2,1)}, u32[]{:S(2)}) copy-start(bf16[256,1536]{1,0:T(8,128)(2,1)} %x_ref.1) | copy-start | bytes 2359300
  1.8 0.7 copy-start.1
  2.4 0.7 copy-start.2

commit v7 on v6

--- a/solution.py
+++ b/solution.py
@@ -46,7 +46,9 @@
     short_ref, owner_ref, x_ref, w_ref,
     att_ref, lse_ref, kv_ref,
     wbuf, xbuf, proj, cosine, sine, qkv, rows, outbox, inbuf, late, krow, near, obuf, lbuf, local, logged, tops,
+    ask, aid, aid_log, aided, aided_log,
     wsem, xown, xsend, xrecv, lsend, lrecv, nsend, nrecv, csend, crecv, asend, arecv, msend, mrecv,
+    hsend, hrecv,
 ):
     me = lax.axis_index("seq")
     core = lax.axis_index("head")
@@ -58,7 +60,7 @@
     group_heads = heads // groups
     n_real = n_long + n_seq // 4
     n_early = inbuf.shape[0]
-    last_slot = n_long - n_early - 2
+    helper = n_long - 2
     half = n_seq // 2
 
     def weight_copy(c):
@@ -264,31 +266,32 @@
             device_id_type=MESH,
         )
 
-    def relay_copy():
+    def help_copy(i):
+        src, dst, target = (
+            (qkv.at[:, pl.ds(0, HD)], ask, helper),
+            (aid, aided, n_long - 1),
+            (aid_log, aided_log, n_long - 1),
+        )[i]
         return pltpu.make_async_remote_copy(
-            src_ref=near.at[0],
-            dst_ref=near.at[last_slot],
-            send_sem=nsend.at[last_slot],
-            recv_sem=nrecv.at[last_slot],
-            device_id={"seq": n_long - 1},
+            src_ref=src,
+            dst_ref=dst,
+            send_sem=hsend.at[i],
+            recv_sem=hrecv.at[i],
+            device_id={"seq": target},
             device_id_type=MESH,
         )
 
+    @pl.when(me == n_long - 1)
+    def _():
+        help_copy(0).start()
+
     feeds_short = (me >= n_long) & (me < n_real - 1)
 
-    @pl.when(is_late)
+    @pl.when(is_late & (me < helper))
     def _():
         @pl.loop(me + 1, n_long)
         def _(d):
-            relayed = (me == n_long - 2) & (d == n_long - 1)
-
-            @pl.when(relayed)
-            def _():
-                near_copy(n_long, 0, 0).start()
-
-            @pl.when(jnp.logical_not(relayed))
-            def _():
-                near_copy(d, me - n_early, d - me - 1).start()
+            near_copy(d, me - n_early, d - me - 1).start()
 
     @pl.when(feeds_short)
     def _():
@@ -389,14 +392,10 @@
             for copy in answer_copies(j, me):
                 copy.start()
 
-    @pl.when(me == n_long)
-    def _():
-        near_copy(0, 0, 0).wait_recv()
-        relay_copy().start()
-
     @pl.when(is_late | is_short)
     def _():
-        slots = jnp.where(is_late, me - n_early, jnp.where(me > n_long, 1, 0))
+        late_slots = jnp.minimum(me, helper) - n_early
+        slots = jnp.where(is_late, late_slots, jnp.where(me > n_long, 1, 0))
 
         def keep(h, state):
             tops[h], logged[h], local[h] = state
@@ -406,6 +405,20 @@
             here = jnp.dot(qkv[h, HD:2 * HD, :].T, qkv[h, :HD, :], preferred_element_type=F32)
             here = jnp.where((key_iota <= query_iota) & (key_iota >= begin), here, LOW)
             keep(h, first(here, qkv[h, 2 * HD:, :]))
+
+        @pl.when(me == helper)
+        def _():
+            help_copy(0).wait_recv()
+
+            @pl.loop(0, heads)
+            def _(h):
+                scores = jnp.dot(qkv[h, HD:2 * HD, :].T, ask[h], preferred_element_type=F32)
+                top, total, context = first(scores, qkv[h, 2 * HD:, :])
+                aid[h] = (context / total).astype(BF16)
+                aid_log[h] = top * SCALE + jnp.log(total)
+
+            help_copy(1).start()
+            help_copy(2).start()
 
         @pl.loop(0, slots)
         def _(slot):
@@ -431,18 +444,29 @@
                 att_ref[h] = jnp.where(padding, 0.0, local[h]).astype(BF16)
                 lse_ref[h] = jnp.where(padding, 0.0, logged[h])
 
+        def merge(h, context_there, logs_there):
+            logs_here = logged[h]
+            most = jnp.maximum(logs_here, logs_there)
+            logs = most + jnp.log(jnp.exp(logs_here - most) + jnp.exp(logs_there - most))
+            merged = local[h] * jnp.exp(logs_here - logs)
+            return merged + context_there.astype(F32) * jnp.exp(logs_there - logs), logs
+
+        @pl.when(me == n_long - 1)
+        def _():
+            help_copy(1).wait_recv()
+            help_copy(2).wait_recv()
+
+            @pl.loop(0, heads)
+            def _(h):
+                local[h], logged[h] = merge(h, aided[h], aided_log[h])
+
         @pl.when(is_late)
         def _():
             @pl.loop(0, heads)
             def _(h):
                 for copy in answer_copies(0, h):
                     copy.wait_recv()
-                logs_here = logged[h]
-                logs_there = lse_ref[h]
-                most = jnp.maximum(logs_here, logs_there)
-                logs = most + jnp.log(jnp.exp(logs_here - most) + jnp.exp(logs_there - most))
-                merged = local[h] * jnp.exp(logs_here - logs)
-                merged = merged + att_ref[h].astype(F32) * jnp.exp(logs_there - logs)
+                merged, logs = merge(h, att_ref[h], lse_ref[h])
                 att_ref[h] = merged.astype(BF16)
                 lse_ref[h] = logs
 
@@ -482,6 +506,8 @@
         def _(h):
             query_copy(h, me).wait_send()
 
+    @pl.when(is_late & (me < helper))
+    def _():
         @pl.loop(me + 1, n_long)
         def _(d):
             near_copy(d, me - n_early, d - me - 1).wait_send()
@@ -490,9 +516,14 @@
     def _():
         near_copy(me + 1, 0, 0).wait_send()
 
-    @pl.when(me == n_long)
-    def _():
-        relay_copy().wait_send()
+    @pl.when(me == n_long - 1)
+    def _():
+        help_copy(0).wait_send()
+
+    @pl.when(me == helper)
+    def _():
+        help_copy(1).wait_send()
+        help_copy(2).wait_send()
 
     @pl.when(me < heads)
     def _():
@@ -533,7 +564,7 @@
     n_early = n_seq // 2
     groups = 2 if heads % 4 == 0 else 1
     group_width = heads // groups * 2 * HD
-    slots = n_long - n_early - 1
+    slots = n_long - n_early - 2
     width = 256 if cols % 256 == 0 else cols
     tiles = cols // width
 
@@ -568,13 +599,18 @@
             pltpu.VMEM((heads, HD, tok), F32),
             pltpu.VMEM((heads, 1, tok), F32),
             pltpu.VMEM((heads, 1, tok), F32),
+            pltpu.VMEM((heads, HD, tok), BF16),
+            pltpu.VMEM((heads, HD, tok), BF16),
+            pltpu.VMEM((heads, 1, tok), F32),
+            pltpu.VMEM((heads, HD, tok), BF16),
+            pltpu.VMEM((heads, 1, tok), F32),
             dma((tiles,)),
             dma,
             dma((n_head - 1,)),
             dma((n_head - 1,)),
             dma((heads,)),
             dma((n_long,)),
-            dma((slots,)),
+            dma((slots + 1,)),
             dma((slots,)),
             dma((groups, n_seq)),
             dma((groups, n_seq)),
@@ -582,6 +618,8 @@
             dma((heads,)),
             dma((n_long,)),
             dma((heads,)),
+            dma((3,)),
+            dma((3,)),
         ],
         compiler_params=pltpu.CompilerParams(
             collective_id=0, has_side_effects=True, vmem_limit_bytes=50 * 1024 * 1024

time: 78.6 us -> 72.4 us (0.921)
  Pallas kernels: 72.6 us -> 66.1 us
    pallas_call x1, Pallas kernels: 72.6 us -> 66.1 us  [body(): pl.pallas_call(functools.partial(kernel, n_seq, n_head, n_long), out_shap...]
where the time goes in v7:
time: 72.4 us; the launch traced here: 71.9 us
  Pallas kernels  66.1 us (91%)
  local copies, waits for them, and re-layouts  5.12 us (7%)
    pallas_call x1, Pallas kernels, body(): pl.pallas_call(functools.partial(kernel, n_seq, n_head, n_long), out_shap...  66.1 us
    unnamed x8, local copies, waits for them, and re-layouts  4.2 us

profile of v7, /device:TPU:20, one launch (start us, length us, event | category | flops | bytes accessed | tf_op | source)
XLA Modules:
  0.0 71.9 jit_solution(2129691445879639932)
XLA Ops:
  0.6 0.0 copy-start
  0.6 1.1 %copy-done = bf16[256,1536]{1,0:T(8,128)(2,1)S(1)} copy-done((bf16[256,1536]{1,0:T(8,128)(2,1)S(1)}, bf16[256,1536]{1,0:T(8,128)(2,1)}, u32[]{:S(2)}) %copy-start) | copy-done | bytes 786456
  1.8 0.0 copy-start.1
  1.8 0.7 copy-done.1
  2.4 0.0 copy-start.2
  2.4 0.7 copy-done.2
  3.1 66.1 %shard_map.67 = (bf16[8,96,256]{2,1,0:T(8,128)(2,1)S(1)}, f32[8,1,256]{2,1,0:T(1,128)S(1)}, bf16[16,32,1536]{2,1,0:T(8,128)(2,1)S(1)}) custom-call(s32[8]{0:T(128)S(1)} %copy-done.2, s32[256]{0:T(256)S(1)} %bitcast.9, bf16[256,1536]{1,0:T(8,128)(2,1)S(1)} %copy-done, bf16[3072,2304]{1,0:T(8,128)(2,1)} %w_ref.1), custom_call_target="tpu_custom_call" | custom-call | flops 3623878656 | bytes 14155776 | tf_op jit(solution)/shard_map/pallas_call | solution.py:575
  69.2 0.9 %copy.7 = bf16[768,256]{0,1:T(8,128)(2,1)} copy(bf16[768,256]{1,0:T(8,128)(2,1)S(1)} %bitcast.8) | data formatting | bytes 786432 | tf_op jit(solution)/shard_map/reshape | solution.py:634
  70.2 0.6 copy.10
  70.8 1.1 %copy.12 = bf16[512,1536]{1,0:T(8,128)(2,1)} copy(bf16[512,1536]{1,0:T(8,128)(2,1)S(1)} %bitcast.7) | data formatting | bytes 3145728
Async XLA Ops:
  0.6 1.1 %copy-start = (bf16[256,1536]{1,0:T(8,128)(2,1)S(1)}, bf16[256,1536]{1,0:T(8,128)(2,1)}, u32[]{:S(2)}) copy-start(bf16[256,1536]{1,0:T(8,128)(2,1)} %x_ref.1) | copy-start | bytes 2359300
  1.8 0.7 copy-start.1
  2.4 0.7 copy-start.2

commit v8 on v7

--- a/solution.py
+++ b/solution.py
@@ -45,7 +45,7 @@
     n_seq, n_head, n_long,
     short_ref, owner_ref, x_ref, w_ref,
     att_ref, lse_ref, kv_ref,
-    wbuf, xbuf, proj, cosine, sine, qkv, rows, outbox, inbuf, late, krow, near, obuf, lbuf, local, logged, tops,
+    wbuf, xbuf, acc, proj, cosine, sine, qkv, rows, outbox, inbuf, late, krow, near, obuf, lbuf, local, logged, tops,
     ask, aid, aid_log, aided, aided_log,
     wsem, xown, xsend, xrecv, lsend, lrecv, nsend, nrecv, csend, crecv, asend, arecv, msend, mrecv,
     hsend, hrecv,
@@ -131,6 +131,17 @@
     for r in range(1, n_head):
         feature_copy(r).start()
     own_features.wait()
+
+    def product(c, r):
+        peer = lax.rem(core + r, n_head)
+        weights = wbuf[c, pl.ds(pl.multiple_of(peer * feat, 128), feat), :]
+        return jnp.dot(xbuf[peer], weights, preferred_element_type=F32)
+
+    @pl.loop(0, tiles)
+    def _(c):
+        weight_copy(c).wait()
+        acc[c] = product(c, 0)
+
     for r in range(1, n_head):
         feature_arrival(r).wait_recv()
 
@@ -158,12 +169,9 @@
     is_short = (me >= n_long) & (me < n_real)
 
     def project(c):
-        weight_copy(c).wait()
-        part = jnp.zeros((tok, width), F32)
-        for r in range(n_head):
-            part = part + jnp.dot(
-                xbuf[r], wbuf[c, r * feat:(r + 1) * feat, :], preferred_element_type=F32
-            )
+        part = acc[c]
+        for r in range(1, n_head):
+            part = part + product(c, r)
         proj[pl.ds(pl.multiple_of(c * width, 8), width), :] = part.T
 
         @pl.loop(c * width // PART, (c + 1) * width // PART)
@@ -584,6 +592,7 @@
         scratch_shapes=[
             pltpu.VMEM((tiles, n_head * feat, width), BF16),
             pltpu.VMEM((n_head, tok, feat), BF16),
+            pltpu.VMEM((tiles, tok, width), F32),
             pltpu.VMEM((cols, tok), F32),
             pltpu.VMEM((HALF, tok), F32),
             pltpu.VMEM((HALF, tok), F32),

time: 72.4 us -> 67.7 us (0.935)
  Pallas kernels: 66.1 us -> 61.8 us
    pallas_call x1, Pallas kernels: 66.1 us -> 61.8 us  [body(): pl.pallas_call(functools.partial(kernel, n_seq, n_head, n_long), out_shap...]
where the time goes in v8:
time: 67.7 us; the launch traced here: 67.5 us
  Pallas kernels  61.8 us (91%)
  local copies, waits for them, and re-layouts  5.12 us (8%)
    pallas_call x1, Pallas kernels, body(): pl.pallas_call(functools.partial(kernel, n_seq, n_head, n_long), out_shap...  61.8 us
    unnamed x8, local copies, waits for them, and re-layouts  4.2 us

profile of v8, /device:TPU:20, one launch (start us, length us, event | category | flops | bytes accessed | tf_op | source)
XLA Modules:
  0.0 67.5 jit_solution(18185461182329821825)
XLA Ops:
  0.6 0.0 copy-start
  0.6 1.1 %copy-done = bf16[256,1536]{1,0:T(8,128)(2,1)S(1)} copy-done((bf16[256,1536]{1,0:T(8,128)(2,1)S(1)}, bf16[256,1536]{1,0:T(8,128)(2,1)}, u32[]{:S(2)}) %copy-start) | copy-done | bytes 786456
  1.8 0.0 copy-start.1
  1.8 0.7 %copy-done.1 = s32[256,1]{0,1:T(1,128)S(1)} copy-done((s32[256,1]{0,1:T(1,128)S(1)}, s32[256,1]{0,1:T(1,128)}, u32[]{:S(2)}) %copy-start.1) | copy-done | bytes 1048
  2.4 0.0 copy-start.2
  2.4 0.7 copy-done.2
  3.1 61.8 %shard_map.67 = (bf16[8,96,256]{2,1,0:T(8,128)(2,1)S(1)}, f32[8,1,256]{2,1,0:T(1,128)S(1)}, bf16[16,32,1536]{2,1,0:T(8,128)(2,1)S(1)}) custom-call(s32[8]{0:T(128)S(1)} %copy-done.2, s32[256]{0:T(256)S(1)} %bitcast.9, bf16[256,1536]{1,0:T(8,128)(2,1)S(1)} %copy-done, bf16[3072,2304]{1,0:T(8,128)(2,1)} %w_ref.1), custom_call_target="tpu_custom_call" | custom-call | flops 3623878656 | bytes 14155776 | tf_op jit(solution)/shard_map/pallas_call | solution.py:583
  64.9 0.9 %copy.7 = bf16[768,256]{0,1:T(8,128)(2,1)} copy(bf16[768,256]{1,0:T(8,128)(2,1)S(1)} %bitcast.8) | data formatting | bytes 786432 | tf_op jit(solution)/shard_map/reshape | solution.py:643
  65.8 0.6 copy.10
  66.4 1.1 %copy.12 = bf16[512,1536]{1,0:T(8,128)(2,1)} copy(bf16[512,1536]{1,0:T(8,128)(2,1)S(1)} %bitcast.7) | data formatting | bytes 3145728
Async XLA Ops:
  0.6 1.1 %copy-start = (bf16[256,1536]{1,0:T(8,128)(2,1)S(1)}, bf16[256,1536]{1,0:T(8,128)(2,1)}, u32[]{:S(2)}) copy-start(bf16[256,1536]{1,0:T(8,128)(2,1)} %x_ref.1) | copy-start | bytes 2359300
  1.8 0.7 %copy-start.1 = (s32[256,1]{0,1:T(1,128)S(1)}, s32[256,1]{0,1:T(1,128)}, u32[]{:S(2)}) copy-start(s32[256,1]{0,1:T(1,128)} %param.7) | copy-start | bytes 3076
  2.4 0.7 copy-start.2

commit v9 on v8

--- a/solution.py
+++ b/solution.py
@@ -570,7 +570,7 @@
     cap = 2 * tok // n_seq
     pages = tok // cap
     n_early = n_seq // 2
-    groups = 2 if heads % 4 == 0 else 1
+    groups = max(heads // 2, 1)
     group_width = heads // groups * 2 * HD
     slots = n_long - n_early - 2
     width = 256 if cols % 256 == 0 else cols

time: 67.7 us -> 75.3 us (1.11)
  Pallas kernels: 61.8 us -> 69.3 us
    pallas_call x1, Pallas kernels: 61.8 us -> 69.3 us  [body(): pl.pallas_call(functools.partial(kernel, n_seq, n_head, n_long), out_shap...]
where the time goes in v9:
time: 75.3 us; the launch traced here: 75.1 us
  Pallas kernels  69.3 us (92%)
  local copies, waits for them, and re-layouts  5.12 us (7%)
    pallas_call x1, Pallas kernels, body(): pl.pallas_call(functools.partial(kernel, n_seq, n_head, n_long), out_shap...  69.3 us
    unnamed x8, local copies, waits for them, and re-layouts  4.2 us

profile of v9, /device:TPU:20, one launch (start us, length us, event | category | flops | bytes accessed | tf_op | source)
XLA Modules:
  0.0 75.1 jit_solution(3054005105747534461)
XLA Ops:
  0.6 0.0 copy-start
  0.6 1.1 %copy-done = bf16[256,1536]{1,0:T(8,128)(2,1)S(1)} copy-done((bf16[256,1536]{1,0:T(8,128)(2,1)S(1)}, bf16[256,1536]{1,0:T(8,128)(2,1)}, u32[]{:S(2)}) %copy-start) | copy-done | bytes 786456
  1.8 0.0 copy-start.1
  1.8 0.7 copy-done.1
  2.4 0.0 copy-start.2
  2.4 0.7 copy-done.2
  3.1 69.3 %shard_map.67 = (bf16[8,96,256]{2,1,0:T(8,128)(2,1)S(1)}, f32[8,1,256]{2,1,0:T(1,128)S(1)}, bf16[16,32,1536]{2,1,0:T(8,128)(2,1)S(1)}) custom-call(s32[8]{0:T(128)S(1)} %copy-done.2, s32[256]{0:T(256)S(1)} %bitcast.9, bf16[256,1536]{1,0:T(8,128)(2,1)S(1)} %copy-done, bf16[3072,2304]{1,0:T(8,128)(2,1)} %w_ref.1), custom_call_target="tpu_custom_call" | custom-call | flops 3623878656 | bytes 14155776 | tf_op jit(solution)/shard_map/pallas_call | solution.py:583
  72.4 0.9 %copy.7 = bf16[768,256]{0,1:T(8,128)(2,1)} copy(bf16[768,256]{1,0:T(8,128)(2,1)S(1)} %bitcast.8) | data formatting | bytes 786432 | tf_op jit(solution)/shard_map/reshape | solution.py:643
  73.4 0.6 copy.10
  74.0 1.1 %copy.12 = bf16[512,1536]{1,0:T(8,128)(2,1)} copy(bf16[512,1536]{1,0:T(8,128)(2,1)S(1)} %bitcast.7) | data formatting | bytes 3145728
Async XLA Ops:
  0.6 1.1 %copy-start = (bf16[256,1536]{1,0:T(8,128)(2,1)S(1)}, bf16[256,1536]{1,0:T(8,128)(2,1)}, u32[]{:S(2)}) copy-start(bf16[256,1536]{1,0:T(8,128)(2,1)} %x_ref.1) | copy-start | bytes 2359300
  1.8 0.7 copy-start.1
  2.4 0.7 copy-start.2
